TPU v7x, 512 devices: a whole 4x4x16 slice. The times are simulated.
512 devices in a mesh: leaf: 128 (over z, y, core), rhs: 4 (over x).
Axes of the slice: x: 4, y: 4, z: 16, core: 2. Of those that a mesh axis runs over, the one named last changes fastest.
Arguments:
- vectors: bfloat16 [64, 262144], P('rhs', 'leaf'), may hold values from -6 to 6
- near_blocks: bfloat16 [16, 2048, 128, 128], P('rhs', 'leaf'), may hold values from -0.125 to 0.125
- near_src: int32 [16, 2048], P('rhs', 'leaf'), may hold values from 0 to 2047, as said below
- basis: bfloat16 [2048, 64, 128], P('leaf'), may hold values from -0.5 to 0.5
- local_transfer: bfloat16 [1920, 64, 128], P('leaf'), may hold values from -0.625 to 0.625
- leaf_coupling: bfloat16 [2048, 64, 384], P('leaf'), may hold values from -0.3125 to 0.3125
- far_slot: int32 [2048, 6], P('leaf'), may hold values from 0 to 143, as said below
- want_leaf: int32 [128, 128], replicated, may hold values from 0 to 15
- top_transfer: bfloat16 [128, 6, 64, 128], P('leaf'), as said below
- top_coupling: bfloat16 [128, 7, 64, 128], P('leaf'), as said below
Outputs:
- result_vectors: float32 [64, 262144], P('rhs', 'leaf')
Inputs may be any that keep to these rules, and one draw needn't show every extreme that they name: near_src[0, t] = t; every entry of column t lies within 16 leaves of t; entries of one column may repeat. `far_slot`: entries below 16 give a leaf of the target's own device by its local index; entry 16 + p stands for the leaf that the target's device requests from device p in want_leaf, where p is never the target's own device; for every leaf the device p of far pair 2 lies 128 / 2 devices away counted round, and those of its other remote pairs lie within 3 devices. top_transfer[d, j - 1] is the transfer matrix of the level-j ancestor of device d's root; all 2**j devices under one ancestor hold equal copies. top_coupling[d, j - 1] holds the two sibling coupling matrices of the level-j ancestor of device d's root; all 2**j devices under one ancestor hold equal copies.
All inputs are finite; a program needn't handle non-finite values.
Results may differ from a plain program's by a relative error of at most 0.029.
Values may be sent and summed in bfloat16 or wider, within the bound.
A program may use at most 128 MiB of HBM per device.

v0:
```python
import jax
import jax.numpy as jnp
from jax import lax
from jax.sharding import PartitionSpec as P


def padded(array, sides, width):
    for axis, dim in sides:
        devices, length = (lax.axis_size(axis), array.shape[dim])
        up = [(i, (i + 1) % devices) for i in range(devices - 1)]
        down = [(j, i) for i, j in up]
        last = lax.slice_in_dim(array, length - width, length, axis=dim)
        first = lax.slice_in_dim(array, 0, width, axis=dim)
        before = lax.ppermute(last, axis, up)
        after = lax.ppermute(first, axis, down)
        array = jnp.concatenate([before, array, after], axis=dim)
    return array


def from_behind(array, axis, by):
    devices = lax.axis_size(axis)
    pairs = [(i, i + by) for i in range(devices) if 0 <= i + by < devices]
    return lax.ppermute(array, axis, pairs)


def near_terms(window, blocks, sources, window_start):
    row_count = window.shape[0]
    leaf_size = blocks.shape[-1]
    leaves = window.reshape(row_count, -1, leaf_size)
    picked = jnp.take(leaves, sources - window_start, axis=1)
    return jnp.einsum("qtij,vqtj->vti", blocks, picked, preferred_element_type=jnp.float32)


def local_level(local_transfer, leaves_here, height):
    count_now = leaves_here >> height
    start_at = leaves_here - (leaves_here >> height - 1)
    return local_transfer[start_at : start_at + count_now]


def lift_pair(matrix, left_up, right_up):
    stacked = jnp.concatenate([left_up, right_up], axis=1)
    return jnp.einsum("km,vm->vk", matrix, stacked, preferred_element_type=jnp.float32).astype(
        jnp.bfloat16
    )


def spread_down(matrix, down_now):
    return jnp.einsum("km,vk->vm", matrix, down_now, preferred_element_type=jnp.float32)


def couple(matrix, source):
    return jnp.einsum("km,vm->vk", matrix, source, preferred_element_type=jnp.float32)


def local(
    vectors,
    near_blocks,
    near_src,
    basis,
    local_transfer,
    leaf_coupling,
    far_slot,
    want_leaf,
    top_transfer,
    top_coupling,
):
    vec_rows, span_cols = vectors.shape
    leaves_here, rank_dim, leaf_size = basis.shape
    device = lax.axis_index("leaf")
    window_start = (device - 1) * leaves_here
    window = padded(vectors, (("leaf", 1),), span_cols)
    near_part = near_terms(
        window,
        lax.all_gather(near_blocks, "rhs", axis=0, tiled=True),
        lax.all_gather(near_src, "rhs", axis=0, tiled=True),
        window_start,
    ).reshape(vec_rows, span_cols)
    points = vectors.reshape(vec_rows, leaves_here, leaf_size)
    up_zero = jnp.einsum("tkp,vtp->vtk", basis, points, preferred_element_type=jnp.float32).astype(
        jnp.bfloat16
    )
    levels_here = leaves_here.bit_length() - 1
    coeffs = up_zero
    for height in range(1, levels_here + 1):
        matrices = local_level(local_transfer, leaves_here, height)
        paired = coeffs.reshape(vec_rows, -1, 2 * rank_dim)
        coeffs = jnp.einsum(
            "ckm,vcm->vck", matrices, paired, preferred_element_type=jnp.float32
        ).astype(jnp.bfloat16)
    root_up = coeffs.reshape(vec_rows, rank_dim)
    senders = lax.axis_size("leaf")
    gathered_all = lax.all_gather(
        up_zero.reshape(vec_rows, leaves_here * rank_dim), "leaf", axis=1, tiled=True
    )
    wanted = jnp.arange(senders, dtype=jnp.int32) * leaves_here + lax.dynamic_index_in_dim(
        want_leaf, device, 0, keepdims=False
    )
    remote = jnp.take(
        gathered_all.reshape(vec_rows, senders * leaves_here, rank_dim), wanted, axis=1
    )
    source_pool = jnp.concatenate([up_zero, remote], axis=1)
    far_sources = jnp.take(source_pool, far_slot.reshape(-1), axis=1).reshape(
        vec_rows, leaves_here, -1
    )
    coupled = jnp.einsum(
        "tkm,vtm->vtk", leaf_coupling, far_sources, preferred_element_type=jnp.float32
    )
    top_levels = senders.bit_length() - 1
    top_up = top_transfer[0]
    mixing = top_coupling[0]
    left_list = []
    right_list = []
    node_up = root_up
    for height in range(1, top_levels + 1):
        right_up = from_behind(node_up, "leaf", -(1 << height - 1))
        left_list.append(node_up)
        right_list.append(right_up)
        if height < top_levels:
            node_up = lift_pair(top_up[height - 1], node_up, right_up)
    down_now = None
    for height in range(top_levels, 0, -1):
        half_span = 1 << height - 1
        left_sum = couple(mixing[height - 1][:, :rank_dim], right_list[height - 1])
        right_sum = couple(mixing[height - 1][:, rank_dim:], left_list[height - 1])
        if down_now is not None:
            spread = spread_down(top_up[height - 1], down_now)
            left_sum = left_sum + spread[:, :rank_dim]
            right_sum = right_sum + spread[:, rank_dim:]
        left_down = left_sum.astype(jnp.bfloat16)
        right_down = right_sum.astype(jnp.bfloat16)
        moved = from_behind(right_down, "leaf", half_span)
        down_now = jnp.where(device % (2 * half_span) == half_span, moved, left_down)
    down_now = down_now.reshape(vec_rows, 1, rank_dim)
    spread = None
    for height in range(levels_here, 0, -1):
        matrices = local_level(local_transfer, leaves_here, height)
        spread = jnp.einsum(
            "ckm,vck->vcm", matrices, down_now, preferred_element_type=jnp.float32
        ).reshape(vec_rows, -1, rank_dim)
        if height > 1:
            down_now = spread.astype(jnp.bfloat16)
    down_zero = (spread + coupled).astype(jnp.bfloat16)
    far_part = jnp.einsum(
        "tkp,vtk->vtp", basis, down_zero, preferred_element_type=jnp.float32
    ).reshape(vec_rows, span_cols)
    return near_part + far_part


def solution(mesh):
    in_specs = (
        P("rhs", "leaf"),
        P("rhs", "leaf", None, None),
        P("rhs", "leaf"),
        P("leaf", None, None),
        P("leaf", None, None),
        P("leaf", None, None),
        P("leaf", None),
        P(),
        P("leaf", None, None, None),
        P("leaf", None, None, None),
    )
    out_specs = P("rhs", "leaf")
    return jax.shard_map(local, mesh=mesh, in_specs=in_specs, out_specs=out_specs, check_vma=False)
```

profile of v0, /device:TPU:1, one launch (start us, length us, event | category | flops | bytes accessed | tf_op | source)
XLA Modules:
  0.0 259.5 jit_solution(6593647977637991180)
XLA Ops:
  6.5 1.3 fusion.3
  7.9 0.7 reshape.165
  8.7 0.7 all-gather.4.cloned.1.call-update
  9.5 1.1 fusion.4
  10.7 1.0 fusion.5
  11.8 0.9 fusion.7
  12.8 0.8 convolution_convert_fusion.15
  13.6 8.8 %collective-permute-start.2 = (bf16[16,64]{1,0:T(8,128)(2,1)S(1)}, bf16[16,64]{1,0:T(8,128)(2,1)S(1)}, u32[]{:S(2)}, u32[]{:S(2)}) collective-permute-start(bf16[16,64]{1,0:T(8,128)(2,1)S(1)} %convolution_convert_fusion.15), channel_id=1, source_target_pairs={{4,0},{8,4},{12,8},{16,12},{20,16},{24,20},{28,24},{32,28},{36,32}... | collective-permute-start | bytes 6152 | tf_op jit(solution)/shard_map/ppermute | solution.py:23
  22.4 1.9 collective-permute-start
  24.3 2.4 collective-permute-start.1
  26.7 0.9 convolution_convert_fusion.14
  27.7 1.3 collective-permute-start.3
  28.9 0.8 slice_bitcast_fusion
  29.8 2.2 collective-permute-done.3
  32.0 0.9 convolution_convert_fusion.13
  32.9 1.3 collective-permute-start.4
  34.2 0.7 slice_bitcast_fusion.7
  34.9 8.6 %all-gather = s32[4,4,16]{2,1,0:T(4,128)S(1)} all-gather(s32[1,4,16]{2,1,0:T(4,128)} %bitcast.145), channel_id=1, replica_groups=mesh['leaf'=128,'rhs'=4] {'rhs'}, dimensions={0}, use_global_device_ids=true | all-gather | bytes 1280 | tf_op jit(solution)/shard_map/all_gather | solution.py:75
  43.5 0.9 convolution_convert_fusion.12
  44.4 1.3 collective-permute-start.5
  45.8 4.2 %collective-permute-done.5 = bf16[16,64]{1,0:T(8,128)(2,1)S(1)} collective-permute-done((bf16[16,64]{1,0:T(8,128)(2,1)S(1)}, bf16[16,64]{1,0:T(8,128)(2,1)S(1)}, u32[]{:S(2)}, u32[]{:S(2)}) %collective-permute-start.5) | collective-permute-done | bytes 2080 | tf_op jit(solution)/shard_map/ppermute | solution.py:23
  49.9 0.9 convolution_convert_fusion.11
  50.8 1.3 collective-permute-start.6
  52.1 5.0 %collective-permute-done.6 = bf16[16,64]{1,0:T(8,128)(2,1)S(1)} collective-permute-done((bf16[16,64]{1,0:T(8,128)(2,1)S(1)}, bf16[16,64]{1,0:T(8,128)(2,1)S(1)}, u32[]{:S(2)}, u32[]{:S(2)}) %collective-permute-start.6) | collective-permute-done | bytes 2080 | tf_op jit(solution)/shard_map/ppermute | solution.py:23
  57.2 0.9 convolution_convert_fusion.10
  58.1 1.3 collective-permute-start.7
  59.4 8.6 %collective-permute-done.7 = bf16[16,64]{1,0:T(8,128)(2,1)S(1)} collective-permute-done((bf16[16,64]{1,0:T(8,128)(2,1)S(1)}, bf16[16,64]{1,0:T(8,128)(2,1)S(1)}, u32[]{:S(2)}, u32[]{:S(2)}) %collective-permute-start.7) | collective-permute-done | bytes 2080 | tf_op jit(solution)/shard_map/ppermute | solution.py:23
  67.9 0.9 convolution_convert_fusion.9
  68.8 1.3 collective-permute-start.9
  70.3 14.2 %collective-permute-start.8 = (bf16[16,64]{1,0:T(8,128)(2,1)S(1)}, bf16[16,64]{1,0:T(8,128)(2,1)S(1)}, u32[]{:S(2)}, u32[]{:S(2)}) collective-permute-start(bf16[16,64]{1,0:T(8,128)(2,1)S(1)} %convolution_convert_fusion.8), channel_id=1, source_target_pairs={{0,256},{4,260},{8,264},{12,268},{16,272},{20,276},{24,280},{28,28... | collective-permute-start | bytes 6152 | tf_op jit(solution)/shard_map/ppermute | solution.py:23
  84.6 0.7 compare_and_fusion.1
  85.3 0.8 copy.79
  86.1 1.0 fusion.16
  87.3 7.6 %collective-permute-start.10 = (bf16[16,64]{1,0:T(8,128)(2,1)S(1)}, bf16[16,64]{1,0:T(8,128)(2,1)S(1)}, u32[]{:S(2)}, u32[]{:S(2)}) collective-permute-start(bf16[16,64]{1,0:T(8,128)(2,1)S(1)} %fusion.110), channel_id=1, source_target_pairs={{0,128},{4,132},{8,136},{12,140},{16,144},{20,148},{24,152},{28,15... | collective-permute-start | bytes 6152 | tf_op jit(solution)/shard_map/ppermute | solution.py:23
  94.9 0.7 collective-permute-done.10
  95.7 1.0 fusion.28
  96.8 4.8 %collective-permute-start.11 = (bf16[16,64]{1,0:T(8,128)(2,1)S(1)}, bf16[16,64]{1,0:T(8,128)(2,1)S(1)}, u32[]{:S(2)}, u32[]{:S(2)}) collective-permute-start(bf16[16,64]{1,0:T(8,128)(2,1)S(1)} %fusion.108), channel_id=1, source_target_pairs={{0,64},{4,68},{8,72},{12,76},{16,80},{20,84},{24,88},{28,92},{32,9... | collective-permute-start | bytes 6152 | tf_op jit(solution)/shard_map/ppermute | solution.py:23
  101.6 0.7 fusion.136
  102.4 1.0 fusion.26
  103.5 3.9 %collective-permute-start.12 = (bf16[16,64]{1,0:T(8,128)(2,1)S(1)}, bf16[16,64]{1,0:T(8,128)(2,1)S(1)}, u32[]{:S(2)}, u32[]{:S(2)}) collective-permute-start(bf16[16,64]{1,0:T(8,128)(2,1)S(1)} %fusion.106), channel_id=1, source_target_pairs={{0,32},{4,36},{8,40},{12,44},{16,48},{20,52},{24,56},{28,60},{32,6... | collective-permute-start | bytes 6152 | tf_op jit(solution)/shard_map/ppermute | solution.py:23
  107.5 0.7 collective-permute-done.12
  108.2 1.0 fusion.24
  109.3 3.5 %collective-permute-start.13 = (bf16[16,64]{1,0:T(8,128)(2,1)S(1)}, bf16[16,64]{1,0:T(8,128)(2,1)S(1)}, u32[]{:S(2)}, u32[]{:S(2)}) collective-permute-start(bf16[16,64]{1,0:T(8,128)(2,1)S(1)} %fusion.104), channel_id=1, source_target_pairs={{0,16},{4,20},{8,24},{12,28},{16,32},{20,36},{24,40},{28,44},{32,4... | collective-permute-start | bytes 6152 | tf_op jit(solution)/shard_map/ppermute | solution.py:23
  112.9 0.6 collective-permute-done.13
  113.6 1.0 fusion.22
  114.7 5.0 %collective-permute-start.14 = (bf16[16,64]{1,0:T(8,128)(2,1)S(1)}, bf16[16,64]{1,0:T(8,128)(2,1)S(1)}, u32[]{:S(2)}, u32[]{:S(2)}) collective-permute-start(bf16[16,64]{1,0:T(8,128)(2,1)S(1)} %fusion.102), channel_id=1, source_target_pairs={{0,8},{4,12},{8,16},{12,20},{16,24},{20,28},{24,32},{28,36},{32,40... | collective-permute-start | bytes 6152 | tf_op jit(solution)/shard_map/ppermute | solution.py:23
  119.8 0.7 collective-permute-done.14
  120.5 1.0 fusion.20
  121.6 15.3 %collective-permute-start.15 = (bf16[16,64]{1,0:T(8,128)(2,1)S(1)}, bf16[16,64]{1,0:T(8,128)(2,1)S(1)}, u32[]{:S(2)}, u32[]{:S(2)}) collective-permute-start(bf16[16,64]{1,0:T(8,128)(2,1)S(1)} %fusion.100), channel_id=1, source_target_pairs={{0,4},{4,8},{8,12},{12,16},{16,20},{20,24},{24,28},{28,32},{32,36}... | collective-permute-start | bytes 6152 | tf_op jit(solution)/shard_map/ppermute | solution.py:23
  136.9 0.7 compare_and_fusion.2
  138.2 1.0 fusion.8
  139.3 1.0 fusion.6
  140.4 1.0 convolution_bitcast_fusion.2
  141.6 0.9 copy_bitcast_fusion
  142.5 0.8 gather_fusion
  143.3 15.1 %all-gather.6.cloned.1.call-done = bf16[16,131072]{1,0:T(8,128)(2,1)} async-done(((bf16[16,1024]{1,0:T(8,128)(2,1)}), bf16[16,131072]{1,0:T(8,128)(2,1)}) %all-gather.6.cloned.1.call-update) | async-done | bytes 4194320 | tf_op jit(solution)/shard_map/all_gather | solution.py:92
  158.4 11.2 %reshape.166 = bf16[16,2048,64]{2,1,0:T(8,128)(2,1)} reshape(bf16[16,131072]{1,0:T(8,128)(2,1)} %all-gather.6.cloned.1.call-done) | data formatting | bytes 8388608 | tf_op jit(solution)/shard_map/reshape | solution.py:99
  169.7 10.5 %copy.78 = bf16[16,2048,64]{2,0,1:T(8,128)(2,1)} copy(bf16[16,2048,64]{2,1,0:T(8,128)(2,1)} %reshape.166) | data formatting | bytes 8388608 | tf_op jit(solution)/shard_map/reshape | solution.py:99
  180.2 4.1 %gather_fusion.1 = bf16[128,16,64]{2,1,0:T(8,128)(2,1)S(1)} fusion(bf16[16,2048,64]{2,0,1:T(8,128)(2,1)} %copy.78, s32[1024]{0:T(1024)S(1)} %pad_clamp_fusion.1), kind=kCustom, calls=%fused_computation.1 | custom fusion | bytes 524800 | tf_op jit(solution)/shard_map/jit(_take)/gather | solution.py:98
  184.7 0.7 gather_fusion.2
  185.8 61.0 %all-gather.4.cloned.1.call-done = bf16[16,16,128,128]{3,2,1,0:T(8,128)(2,1)} async-done(((bf16[4,16,128,128]{3,2,1,0:T(8,128)(2,1)}), bf16[16,16,128,128]{3,2,1,0:T(8,128)(2,1)}) %all-gather.4.cloned.1.call-update) | async-done | bytes 8388624 | tf_op jit(solution)/shard_map/all_gather | solution.py:74
  246.8 4.7 %convolution_bitcast_fusion.1 = f32[16,16,128]{2,1,0:T(8,128)S(1)} fusion(bf16[16,16,128,128]{3,2,1,0:T(8,128)(2,1)} %all-gather.4.cloned.1.call-done, bf16[16,16,16,128]{3,2,1,0:T(8,128)(2,1)S(1)} %bitcast.139, pred[16,16]{1,0:T(8,128)(4,1)S(1)} %compare_and_fusion), kind=kOutput, calls=%fused_computation.7 | convolution fusion | flops 134742016 | bytes 9568512 | tf_op jit(solution)/shard_map/qtij,vqtj->vti/dot_general | solution.py:31
  251.5 0.5 fusion.1
  252.0 0.7 copy.110
  (55 shorter events, 3.8 us)
Async XLA Ops:
  6.5 244.9 %copy-start = (bf16[16,64,384]{2,1,0:T(8,128)(2,1)S(1)}, bf16[16,64,384]{2,1,0:T(8,128)(2,1)}, u32[]{:S(2)}) copy-start(bf16[16,64,384]{2,1,0:T(8,128)(2,1)} %param.15) | copy-start | bytes 2359300
  6.5 151.9 %all-gather.6.cloned.1.call-start = ((), (), s32[]{:S(2)}) async-start(), calls=%async_computation.1 | async-start | bytes 4227072 | tf_op jit(solution)/shard_map/all_gather | solution.py:92
  8.6 238.2 %all-gather.4.cloned.1.call-start = ((), (), s32[]{:S(2)}) async-start(), calls=%async_computation | async-start | bytes 10485760 | tf_op jit(solution)/shard_map/all_gather | solution.py:74
  13.6 13.1 %collective-permute-start.2 = (bf16[16,64]{1,0:T(8,128)(2,1)S(1)}, bf16[16,64]{1,0:T(8,128)(2,1)S(1)}, u32[]{:S(2)}, u32[]{:S(2)}) collective-permute-start(bf16[16,64]{1,0:T(8,128)(2,1)S(1)} %convolution_convert_fusion.15), channel_id=1, source_target_pairs={{4,0},{8,4},{12,8},{16,12},{20,16},{24,20},{28,24},{32,28},{36,32}... | collective-permute-start | bytes 6152 | tf_op jit(solution)/shard_map/ppermute | solution.py:23
  22.4 119.2 %collective-permute-start = (bf16[16,2048]{1,0:T(8,128)(2,1)}, bf16[16,2048]{1,0:T(8,128)(2,1)S(1)}, u32[]{:S(2)}, u32[]{:S(2)}) collective-permute-start(bf16[16,2048]{1,0:T(8,128)(2,1)} %param.10), channel_id=1, source_target_pairs={{0,4},{4,8},{8,12},{12,16},{16,20},{20,24},{24,28},{28,32},{32,36}... | collective-permute-start | bytes 196616 | tf_op jit(solution)/shard_map/ppermute | solution.py:14
  24.3 117.3 %collective-permute-start.1 = (bf16[16,2048]{1,0:T(8,128)(2,1)}, bf16[16,2048]{1,0:T(8,128)(2,1)S(1)}, u32[]{:S(2)}, u32[]{:S(2)}) collective-permute-start(bf16[16,2048]{1,0:T(8,128)(2,1)} %param.10), channel_id=1, source_target_pairs={{4,0},{8,4},{12,8},{16,12},{20,16},{24,20},{28,24},{32,28},{36,32}... | collective-permute-start | bytes 196616 | tf_op jit(solution)/shard_map/ppermute | solution.py:15
  27.7 4.3 %collective-permute-start.3 = (bf16[16,64]{1,0:T(8,128)(2,1)S(1)}, bf16[16,64]{1,0:T(8,128)(2,1)S(1)}, u32[]{:S(2)}, u32[]{:S(2)}) collective-permute-start(bf16[16,64]{1,0:T(8,128)(2,1)S(1)} %convolution_convert_fusion.14), channel_id=1, source_target_pairs={{8,0},{12,4},{16,8},{20,12},{24,16},{28,20},{32,24},{36,28},{40,32... | collective-permute-start | bytes 6152 | tf_op jit(solution)/shard_map/ppermute | solution.py:23
  32.9 10.6 %collective-permute-start.4 = (bf16[16,64]{1,0:T(8,128)(2,1)S(1)}, bf16[16,64]{1,0:T(8,128)(2,1)S(1)}, u32[]{:S(2)}, u32[]{:S(2)}) collective-permute-start(bf16[16,64]{1,0:T(8,128)(2,1)S(1)} %convolution_convert_fusion.13), channel_id=1, source_target_pairs={{16,0},{20,4},{24,8},{28,12},{32,16},{36,20},{40,24},{44,28},{48,3... | collective-permute-start | bytes 6152 | tf_op jit(solution)/shard_map/ppermute | solution.py:23
  44.4 5.5 %collective-permute-start.5 = (bf16[16,64]{1,0:T(8,128)(2,1)S(1)}, bf16[16,64]{1,0:T(8,128)(2,1)S(1)}, u32[]{:S(2)}, u32[]{:S(2)}) collective-permute-start(bf16[16,64]{1,0:T(8,128)(2,1)S(1)} %convolution_convert_fusion.12), channel_id=1, source_target_pairs={{32,0},{36,4},{40,8},{44,12},{48,16},{52,20},{56,24},{60,28},{64,3... | collective-permute-start | bytes 6152 | tf_op jit(solution)/shard_map/ppermute | solution.py:23
  50.8 6.3 %collective-permute-start.6 = (bf16[16,64]{1,0:T(8,128)(2,1)S(1)}, bf16[16,64]{1,0:T(8,128)(2,1)S(1)}, u32[]{:S(2)}, u32[]{:S(2)}) collective-permute-start(bf16[16,64]{1,0:T(8,128)(2,1)S(1)} %convolution_convert_fusion.11), channel_id=1, source_target_pairs={{64,0},{68,4},{72,8},{76,12},{80,16},{84,20},{88,24},{92,28},{96,3... | collective-permute-start | bytes 6152 | tf_op jit(solution)/shard_map/ppermute | solution.py:23
  58.1 9.9 %collective-permute-start.7 = (bf16[16,64]{1,0:T(8,128)(2,1)S(1)}, bf16[16,64]{1,0:T(8,128)(2,1)S(1)}, u32[]{:S(2)}, u32[]{:S(2)}) collective-permute-start(bf16[16,64]{1,0:T(8,128)(2,1)S(1)} %convolution_convert_fusion.10), channel_id=1, source_target_pairs={{128,0},{132,4},{136,8},{140,12},{144,16},{148,20},{152,24},{156,2... | collective-permute-start | bytes 6152 | tf_op jit(solution)/shard_map/ppermute | solution.py:23
  68.8 17.3 %collective-permute-start.9 = (bf16[16,64]{1,0:T(8,128)(2,1)S(1)}, bf16[16,64]{1,0:T(8,128)(2,1)S(1)}, u32[]{:S(2)}, u32[]{:S(2)}) collective-permute-start(bf16[16,64]{1,0:T(8,128)(2,1)S(1)} %convolution_convert_fusion.9), channel_id=1, source_target_pairs={{256,0},{260,4},{264,8},{268,12},{272,16},{276,20},{280,24},{284,2... | collective-permute-start | bytes 6152 | tf_op jit(solution)/shard_map/ppermute | solution.py:23
  70.3 15.8 %collective-permute-start.8 = (bf16[16,64]{1,0:T(8,128)(2,1)S(1)}, bf16[16,64]{1,0:T(8,128)(2,1)S(1)}, u32[]{:S(2)}, u32[]{:S(2)}) collective-permute-start(bf16[16,64]{1,0:T(8,128)(2,1)S(1)} %convolution_convert_fusion.8), channel_id=1, source_target_pairs={{0,256},{4,260},{8,264},{12,268},{16,272},{20,276},{24,280},{28,28... | collective-permute-start | bytes 6152 | tf_op jit(solution)/shard_map/ppermute | solution.py:23
  87.3 8.4 %collective-permute-start.10 = (bf16[16,64]{1,0:T(8,128)(2,1)S(1)}, bf16[16,64]{1,0:T(8,128)(2,1)S(1)}, u32[]{:S(2)}, u32[]{:S(2)}) collective-permute-start(bf16[16,64]{1,0:T(8,128)(2,1)S(1)} %fusion.110), channel_id=1, source_target_pairs={{0,128},{4,132},{8,136},{12,140},{16,144},{20,148},{24,152},{28,15... | collective-permute-start | bytes 6152 | tf_op jit(solution)/shard_map/ppermute | solution.py:23
  96.8 5.5 %collective-permute-start.11 = (bf16[16,64]{1,0:T(8,128)(2,1)S(1)}, bf16[16,64]{1,0:T(8,128)(2,1)S(1)}, u32[]{:S(2)}, u32[]{:S(2)}) collective-permute-start(bf16[16,64]{1,0:T(8,128)(2,1)S(1)} %fusion.108), channel_id=1, source_target_pairs={{0,64},{4,68},{8,72},{12,76},{16,80},{20,84},{24,88},{28,92},{32,9... | collective-permute-start | bytes 6152 | tf_op jit(solution)/shard_map/ppermute | solution.py:23
  103.5 4.7 %collective-permute-start.12 = (bf16[16,64]{1,0:T(8,128)(2,1)S(1)}, bf16[16,64]{1,0:T(8,128)(2,1)S(1)}, u32[]{:S(2)}, u32[]{:S(2)}) collective-permute-start(bf16[16,64]{1,0:T(8,128)(2,1)S(1)} %fusion.106), channel_id=1, source_target_pairs={{0,32},{4,36},{8,40},{12,44},{16,48},{20,52},{24,56},{28,60},{32,6... | collective-permute-start | bytes 6152 | tf_op jit(solution)/shard_map/ppermute | solution.py:23
  109.3 4.2 %collective-permute-start.13 = (bf16[16,64]{1,0:T(8,128)(2,1)S(1)}, bf16[16,64]{1,0:T(8,128)(2,1)S(1)}, u32[]{:S(2)}, u32[]{:S(2)}) collective-permute-start(bf16[16,64]{1,0:T(8,128)(2,1)S(1)} %fusion.104), channel_id=1, source_target_pairs={{0,16},{4,20},{8,24},{12,28},{16,32},{20,36},{24,40},{28,44},{32,4... | collective-permute-start | bytes 6152 | tf_op jit(solution)/shard_map/ppermute | solution.py:23
  114.7 5.7 %collective-permute-start.14 = (bf16[16,64]{1,0:T(8,128)(2,1)S(1)}, bf16[16,64]{1,0:T(8,128)(2,1)S(1)}, u32[]{:S(2)}, u32[]{:S(2)}) collective-permute-start(bf16[16,64]{1,0:T(8,128)(2,1)S(1)} %fusion.102), channel_id=1, source_target_pairs={{0,8},{4,12},{8,16},{12,20},{16,24},{20,28},{24,32},{28,36},{32,40... | collective-permute-start | bytes 6152 | tf_op jit(solution)/shard_map/ppermute | solution.py:23
  121.6 16.4 %collective-permute-start.15 = (bf16[16,64]{1,0:T(8,128)(2,1)S(1)}, bf16[16,64]{1,0:T(8,128)(2,1)S(1)}, u32[]{:S(2)}, u32[]{:S(2)}) collective-permute-start(bf16[16,64]{1,0:T(8,128)(2,1)S(1)} %fusion.100), channel_id=1, source_target_pairs={{0,4},{4,8},{8,12},{12,16},{16,20},{20,24},{24,28},{28,32},{32,36}... | collective-permute-start | bytes 6152 | tf_op jit(solution)/shard_map/ppermute | solution.py:23
  180.2 71.3 %copy-start.1 = (bf16[16,64,128]{2,1,0:T(8,128)(2,1)S(1)}, bf16[16,64,128]{2,1,0:T(8,128)(2,1)}, u32[]{:S(2)}) copy-start(bf16[16,64,128]{2,1,0:T(8,128)(2,1)} %param.13) | copy-start | bytes 786436
Sparse Core Ops, SparseCore 0:
  10.5 147.8 all-gather.5
  160.5 86.2 all-gather.3
where the time goes:
time: 262 us; the launch traced here: 260 us
  waiting for transfers between devices  99.6 us (38%)
  starting transfers between devices  75.2 us (29%)
  local copies, waits for them, and re-layouts  32.9 us (13%)
  matrix products  25.9 us (10%)
  between operations  13.9 us (5%)
  blocking collectives  8.62 us (3%)
  other arithmetic  3.37 us (1%)
    ppermute x14, starting transfers between devices, from_behind(): return lax.ppermute(array, axis, pairs)  70.8 us
    all_gather x1, waiting for transfers between devices, local(): lax.all_gather(near_blocks, 'rhs', axis=0, tiled=True)  61 us
    ppermute x14, waiting for transfers between devices, from_behind(): return lax.ppermute(array, axis, pairs)  22.8 us
    reshape x2, local copies, waits for them, and re-layouts, local(): gathered_all.reshape(vec_rows, senders * leaves_here, rank_dim)  21.8 us
    all_gather x1, waiting for transfers between devices, local(): lax.all_gather(up_zero.reshape(vec_rows, leaves_here * rank_dim), 'leaf',...  15.1 us
    all_gather x1, blocking collectives, local(): lax.all_gather(near_src, 'rhs', axis=0, tiled=True)  8.62 us
    dot_general x6, matrix products, spread_down(): jnp.einsum('km,vk->vm', matrix, down_now, preferred_element_type=jnp.floa...  5.75 us
    dot_general x6, matrix products, lift_pair(): jnp.einsum('km,vm->vk', matrix, stacked, preferred_element_type=jnp.float32)  5.41 us
  transfers between devices with their start and end apart: 18, of which 10 were waited for; matrix products, arithmetic and copies ran while one was open for 21% of the time, Pallas kernels for 0%

commit v1 on v0

v1 whole, which is shorter than its diff:
```python
import functools

import jax
import jax.numpy as jnp
from jax import lax
from jax.experimental import pallas as pl
from jax.experimental.pallas import tpu as pltpu
from jax.sharding import PartitionSpec as P

MESH = pl.DeviceIdType.MESH
F32 = jnp.float32
BF16 = jnp.bfloat16
NEAR_CHUNK = 4


def rows_by_rows(lhs, rhs):
    return lax.dot_general(lhs, rhs, (((1,), (1,)), ((), ())), preferred_element_type=F32)


def rows_by_cols(lhs, rhs):
    return lax.dot_general(lhs, rhs, (((1,), (0,)), ((), ())), preferred_element_type=F32)


def twice(matrix):
    return jnp.concatenate([matrix, matrix], axis=0)


def kernel(
    n_leaf,
    n_rhs,
    plane,
    vectors,
    near_blocks,
    near_src,
    basis,
    local_transfer,
    leaf_coupling,
    far_slot,
    want_leaf,
    top_transfer,
    top_coupling,
    out,
    own,
    mine,
    window,
    blocks,
    bases,
    moves,
    couplings,
    top_moves,
    top_couplings,
    src_s,
    far_s,
    want_s,
    leaf_up,
    pool,
    staged,
    message_1,
    arrived_1,
    message_2,
    arrived_2,
    coupled,
    partial,
    others,
    load_sem,
    want_sem,
    gather_send,
    gather_recv,
    side_send,
    side_recv,
    far_send,
    far_recv,
    send_1,
    recv_1,
    send_2,
    recv_2,
    part_send,
    part_recv,
):
    vecs, span = vectors.shape
    leaves, rank, leaf_size = basis.shape
    device = lax.axis_index("leaf")
    row = lax.axis_index("rhs")
    planes = n_leaf // plane
    place = lax.rem(device, plane)
    level = lax.div(device, plane)
    offsets = [1, 2, 3, n_leaf - 1, n_leaf - 2, n_leaf - 3, n_leaf // 2]
    my_rows = pl.ds(pl.multiple_of(row * vecs, vecs), vecs)

    def leaf_at(offset):
        return lax.rem(device + offset, n_leaf)

    def in_plane(where):
        return level * plane + where

    def in_column(where):
        return where * plane + place

    loads = [
        pltpu.make_async_copy(vectors, own, load_sem.at[0]),
        pltpu.make_async_copy(basis, bases, load_sem.at[1]),
        pltpu.make_async_copy(local_transfer, moves, load_sem.at[2]),
        pltpu.make_async_copy(top_transfer.at[0], top_moves, load_sem.at[3]),
        pltpu.make_async_copy(far_slot, far_s, load_sem.at[4]),
        pltpu.make_async_copy(near_src, src_s, load_sem.at[5]),
        pltpu.make_async_copy(near_blocks, blocks, load_sem.at[6]),
        pltpu.make_async_copy(leaf_coupling, couplings, load_sem.at[7]),
        pltpu.make_async_copy(top_coupling.at[0], top_couplings, load_sem.at[8]),
    ]
    wants = [
        pltpu.make_async_copy(
            want_leaf.at[pl.ds(leaf_at(offset), 1)], want_s.at[pl.ds(i, 1)], want_sem.at[i]
        )
        for i, offset in enumerate(offsets)
    ]
    for load in loads + wants:
        load.start()

    barrier = pltpu.get_barrier_semaphore()

    def greet(leaf_index, rhs_index):
        pl.semaphore_signal(
            barrier, inc=1, device_id=(leaf_index, rhs_index), device_id_type=MESH
        )

    for k in range(1, n_rhs):
        greet(device, lax.rem(row + k, n_rhs))
    for offset in offsets:
        greet(leaf_at(offset), row)
    for k in range(1, plane):
        greet(in_plane(lax.rem(place + k, plane)), row)

    def greet_column(k, carry):
        greet(in_column(lax.rem(level + k, planes)), row)
        return carry

    lax.fori_loop(1, planes, greet_column, 0)

    def send(src, dst, send_sem, recv_sem, leaf_index, rhs_index):
        pltpu.make_async_remote_copy(
            src_ref=src,
            dst_ref=dst,
            send_sem=send_sem,
            recv_sem=recv_sem,
            device_id=(leaf_index, rhs_index),
            device_id_type=MESH,
        ).start()

    def wait_bytes(ref, sem):
        pltpu.make_async_copy(ref, ref, sem).wait()

    loads[0].wait()
    points = [own[:, t * leaf_size : (t + 1) * leaf_size] for t in range(leaves)]
    for t in range(leaves):
        mine[t] = points[t]
        window[leaves + t, my_rows] = points[t]
    pl.semaphore_wait(barrier, (n_rhs - 1) + len(offsets) + (plane - 1) + (planes - 1))

    before, centre, after = (pl.ds(i * leaves, leaves) for i in range(3))
    for k in range(1, n_rhs):
        send(
            mine,
            window.at[centre, my_rows],
            gather_send,
            gather_recv.at[k - 1],
            device,
            lax.rem(row + k, n_rhs),
        )
    send(mine, window.at[before, my_rows], side_send.at[0], side_recv.at[0], leaf_at(1), row)
    send(
        mine, window.at[after, my_rows], side_send.at[1], side_recv.at[1], leaf_at(n_leaf - 1), row
    )

    lanes = lax.broadcasted_iota(jnp.int32, (vecs, 2 * rank), 1)
    low = lanes < rank

    def in_half(value, side):
        return jnp.where((lanes >= rank) == (side == 1), value, 0.0).astype(BF16)

    def both(product):
        return jnp.where(low, product[:vecs], product[vecs:])

    def pair_of(ref, node):
        return ref[node : node + 2].reshape(2 * rank, -1)

    loads[1].wait()
    pairs = []
    for c in range(leaves // 2):
        rows = jnp.concatenate([points[2 * c], points[2 * c + 1]], axis=0)
        pair = both(rows_by_rows(rows, pair_of(bases, 2 * c)))
        turned = pltpu.roll(pair, rank, 1)
        for leaf, value in (
            (2 * c, jnp.where(low, pair, turned).astype(BF16)),
            (2 * c + 1, jnp.where(low, turned, pair).astype(BF16)),
        ):
            leaf_up[leaf] = value
            pool[leaf] = value
        pairs.append(pair.astype(BF16))
    loads[2].wait()
    start = 0
    while len(pairs) > 1:
        nodes = len(pairs)
        pairs = [
            both(
                rows_by_rows(
                    jnp.concatenate([pairs[c], pairs[c + 1]], axis=0), pair_of(moves, start + c)
                )
            ).astype(BF16)
            for c in range(0, nodes, 2)
        ]
        start += nodes
    root = rows_by_rows(pairs[0], twice(moves[start]))

    loads[3].wait()
    plane_levels = plane.bit_length() - 1
    column_levels = planes.bit_length() - 1
    top_levels = plane_levels + column_levels

    def side_at(height):
        return lax.rem(lax.div(device, 1 << height - 1), 2)

    def lifted(value, height):
        return rows_by_rows(in_half(value, side_at(height)), twice(top_moves[height - 1]))

    def sibling_start(position, height):
        width = 1 << height - 1
        block = lax.div(position, width)
        return (block + 1 - 2 * lax.rem(block, 2)) * width

    shares = [root]
    for height in range(1, plane_levels + 1):
        shares.append(lifted(shares[-1], height))
    whole_share = shares[plane_levels].astype(BF16)
    for height in range(1, plane_levels + 1):
        message_1[height - 1] = jnp.concatenate(
            [shares[height - 1].astype(BF16), whole_share], axis=1
        )
    arrived_1[place] = message_1[0]
    for height in range(1, plane_levels + 1):
        for i in range(1 << height - 1):
            send(
                message_1.at[height - 1],
                arrived_1.at[place],
                send_1,
                recv_1,
                in_plane(sibling_start(place, height) + i),
                row,
            )

    for i, offset in enumerate(offsets):
        wants[i].wait()
        staged[i] = leaf_up[want_s[i, device]]
        send(
            staged.at[i], pool.at[leaves + device], far_send, far_recv, leaf_at(offset), row
        )

    for k in range(1, n_rhs):
        theirs = pl.ds(pl.multiple_of(lax.rem(row + n_rhs - k, n_rhs) * vecs, vecs), vecs)
        piece = window.at[centre, theirs]
        wait_bytes(piece, gather_recv.at[k - 1])
        send(piece, window.at[before, theirs], side_send.at[0], side_recv.at[0], leaf_at(1), row)
        send(
            piece,
            window.at[after, theirs],
            side_send.at[1],
            side_recv.at[1],
            leaf_at(n_leaf - 1),
            row,
        )

    wait_bytes(arrived_1.at[pl.ds(0, plane - 1)], recv_1)
    siblings = []
    for height in range(1, plane_levels + 1):
        first = sibling_start(place, height)
        siblings.append(
            sum(arrived_1[first + i].astype(F32)[:, : 2 * rank] for i in range(1 << height - 1))
        )
    plane_up = sum(arrived_1[i].astype(F32)[:, 2 * rank :] for i in range(plane))
    share = plane_up
    for height in range(plane_levels + 1, top_levels + 1):
        if height > plane_levels + 1:
            share = lifted(share, height - 1)
        message_2[height - plane_levels - 1] = share.astype(BF16)
    for height in range(1, column_levels + 1):
        first = sibling_start(level, height)

        def send_column(i, carry, height=height, first=first):
            send(
                message_2.at[height - 1],
                arrived_2.at[level],
                send_2,
                recv_2,
                in_column(first + i),
                row,
            )
            return carry

        lax.fori_loop(0, 1 << height - 1, send_column, 0)

    wait_bytes(staged, far_recv)
    loads[4].wait()
    loads[7].wait()

    def far_block(leaf, f):
        return pool[far_s[f, leaf]].astype(F32)

    far = couplings.shape[2] // rank

    def far_row(leaf):
        return jnp.concatenate(
            [
                jnp.where(low, far_block(leaf, f), far_block(leaf, f + 1)).astype(BF16)
                for f in range(0, far, 2)
            ],
            axis=1,
        )

    for c in range(leaves // 2):
        sources = jnp.concatenate([far_row(2 * c), far_row(2 * c + 1)], axis=0)
        coupled[c] = both(rows_by_rows(sources, pair_of(couplings, 2 * c)))

    loads[5].wait()
    loads[6].wait()
    wait_bytes(window.at[before], side_recv.at[0])
    wait_bytes(window.at[after], side_recv.at[1])
    slots = blocks.shape[0]
    first_leaf = (device - 1) * leaves
    width = NEAR_CHUNK * leaf_size
    for chunk in range(leaves // NEAR_CHUNK):
        for leaf in range(chunk * NEAR_CHUNK, (chunk + 1) * NEAR_CHUNK):
            sources = jnp.concatenate(
                [
                    window[(src_s[q, leaf] - first_leaf) & (window.shape[0] - 1)] for q in range(slots)
                ],
                axis=1,
            )
            matrix = jnp.concatenate([blocks[q, leaf] for q in range(slots)], axis=1)
            partial[:, leaf * leaf_size : (leaf + 1) * leaf_size] = rows_by_rows(
                sources, matrix
            ).astype(BF16)
        cols = pl.ds(chunk * width, width)
        for k in range(1, n_rhs):
            target = lax.rem(row + k, n_rhs)
            theirs = pl.ds(pl.multiple_of(target * vecs, vecs), vecs)
            send(
                partial.at[theirs, cols],
                others.at[k - 1, :, cols],
                part_send,
                part_recv,
                device,
                target,
            )

    wait_bytes(arrived_2.at[pl.ds(0, planes - 1)], recv_2)
    for height in range(1, column_levels + 1):
        first = sibling_start(level, height)
        siblings.append(sum(arrived_2[first + i].astype(F32) for i in range(1 << height - 1)))
    loads[8].wait()
    terms = [
        rows_by_rows(in_half(siblings[height - 1], side_at(height)), twice(top_couplings[height - 1]))
        for height in range(1, top_levels + 1)
    ]
    down = in_half(terms[top_levels - 1], side_at(top_levels))
    for height in range(top_levels - 1, 0, -1):
        spread = rows_by_cols(down, twice(top_moves[height - 1]))
        down = in_half(terms[height - 1] + spread, side_at(height))

    def split(pair):
        return jnp.concatenate(
            [jnp.where(low, pair, 0.0), jnp.where(low, 0.0, pair)], axis=0
        ).astype(BF16)

    pairs = [rows_by_cols(down, twice(moves[start]))]
    while len(pairs) < leaves // 2:
        start -= 2 * len(pairs)
        spreads = [
            rows_by_cols(split(pair), pair_of(moves, start + 2 * c))
            for c, pair in enumerate(pairs)
        ]
        pairs = [half for both_now in spreads for half in (both_now[:vecs], both_now[vecs:])]

    wait_bytes(others, part_recv)
    for c, pair in enumerate(pairs):
        far_part = rows_by_cols(split(pair + coupled[c]), pair_of(bases, 2 * c))
        for leaf, value in ((2 * c, far_part[:vecs]), (2 * c + 1, far_part[vecs:])):
            cols = slice(leaf * leaf_size, (leaf + 1) * leaf_size)
            total = value + partial[my_rows, cols].astype(F32)
            for k in range(n_rhs - 1):
                total = total + others[k, :, cols].astype(F32)
            out[:, cols] = total

    if n_rhs > 1:
        wait_bytes(others, gather_send)
        wait_bytes(others, part_send)
    wait_bytes(window.at[before], side_send.at[0])
    wait_bytes(window.at[after], side_send.at[1])
    wait_bytes(staged, far_send)
    wait_bytes(arrived_1.at[pl.ds(0, plane - 1)], send_1)
    wait_bytes(arrived_2.at[pl.ds(0, planes - 1)], send_2)


def local(n_leaf, n_rhs, plane, *arrays):
    (vectors, near_blocks, near_src, basis, local_transfer, leaf_coupling, far_slot) = arrays[:7]
    want_leaf, top_transfer, top_coupling = arrays[7:]
    vecs, span = vectors.shape
    leaves, rank, leaf_size = basis.shape
    far_slot = far_slot.T
    planes = n_leaf // plane
    levels = plane.bit_length() - 1, planes.bit_length() - 1
    dma = pltpu.SemaphoreType.DMA
    scratch = [
        pltpu.VMEM((vecs, span), BF16),
        pltpu.VMEM((leaves, vecs, leaf_size), BF16),
        pltpu.VMEM((4 * leaves, n_rhs * vecs, leaf_size), BF16),
        pltpu.VMEM(near_blocks.shape, BF16),
        pltpu.VMEM(basis.shape, BF16),
        pltpu.VMEM(local_transfer.shape, BF16),
        pltpu.VMEM(leaf_coupling.shape, BF16),
        pltpu.VMEM(top_transfer.shape[1:], BF16),
        pltpu.VMEM(top_coupling.shape[1:], BF16),
        pltpu.SMEM(near_src.shape, jnp.int32),
        pltpu.SMEM(far_slot.shape, jnp.int32),
        pltpu.SMEM((7, n_leaf), jnp.int32),
        pltpu.VMEM((leaves, vecs, 2 * rank), BF16),
        pltpu.VMEM((leaves + n_leaf, vecs, 2 * rank), BF16),
        pltpu.VMEM((7, vecs, 2 * rank), BF16),
        pltpu.VMEM((levels[0], vecs, 4 * rank), BF16),
        pltpu.VMEM((plane, vecs, 4 * rank), BF16),
        pltpu.VMEM((levels[1], vecs, 2 * rank), BF16),
        pltpu.VMEM((planes, vecs, 2 * rank), BF16),
        pltpu.VMEM((leaves // 2, vecs, 2 * rank), F32),
        pltpu.VMEM((n_rhs * vecs, span), BF16),
        pltpu.VMEM((max(n_rhs - 1, 1), vecs, span), BF16),
        dma((9,)),
        dma((7,)),
        dma,
        dma((max(n_rhs - 1, 1),)),
        dma((2,)),
        dma((2,)),
        dma,
        dma,
        dma,
        dma,
        dma,
        dma,
        dma,
        dma,
    ]
    return pl.pallas_call(
        functools.partial(kernel, n_leaf, n_rhs, plane),
        out_shape=jax.ShapeDtypeStruct((vecs, span), F32),
        in_specs=[pl.BlockSpec(memory_space=pltpu.HBM)] * 10,
        out_specs=pl.BlockSpec(memory_space=pltpu.VMEM),
        scratch_shapes=scratch,
        compiler_params=pltpu.CompilerParams(
            collective_id=0, has_side_effects=True, vmem_limit_bytes=60 << 20
        ),
        name="hierarchical_product",
    )(
        vectors,
        near_blocks,
        near_src,
        basis,
        local_transfer,
        leaf_coupling,
        far_slot,
        want_leaf,
        top_transfer,
        top_coupling,
    )


def solution(mesh):
    in_specs = (
        P("rhs", "leaf"),
        P("rhs", "leaf", None, None),
        P("rhs", "leaf"),
        P("leaf", None, None),
        P("leaf", None, None),
        P("leaf", None, None),
        P("leaf", None),
        P(),
        P("leaf", None, None, None),
        P("leaf", None, None, None),
    )
    body = functools.partial(local, mesh.shape["leaf"], mesh.shape["rhs"], 8)
    return jax.shard_map(
        body, mesh=mesh, in_specs=in_specs, out_specs=P("rhs", "leaf"), check_vma=False
    )
```

time: 262 us -> 34.3 us (0.13)
  waiting for transfers between devices: 99.6 us -> 0 us
  starting transfers between devices: 75.2 us -> 0 us
  Pallas kernels: 0 us -> 32.6 us
  local copies, waits for them, and re-layouts: 32.9 us -> 1.57 us
  matrix products: 25.9 us -> 0 us
  between operations: 13.9 us -> 0.01 us
  blocking collectives: 8.62 us -> 0 us
  other arithmetic: 3.37 us -> 0 us
    all_gather x2 -> x0, waiting for transfers between devices: 76.1 us -> none  [the longest x1 61 us: local(): lax.all_gather(near_blocks, 'rhs', axis=0, tiled=True)]
    ppermute x16 -> x0, starting transfers between devices: 75.2 us -> none  [the longest x14 70.8 us: from_behind(): return lax.ppermute(array, axis, pairs)]
    pallas_call x0 -> x1, Pallas kernels: none -> 32.6 us  [local(): pl.pallas_call(functools.partial(kernel, n_leaf, n_rhs, plane), out_shape...]
    dot_general x30 -> x0, matrix products: 25.9 us -> none  [the longest x6 5.75 us: spread_down(): jnp.einsum('km,vk->vm', matrix, down_now, preferred_element_type=jnp.floa...]
    reshape x8 -> x0, local copies, waits for them, and re-layouts: 23 us -> none  [the longest x2 21.8 us: local(): gathered_all.reshape(vec_rows, senders * leaves_here, rank_dim)]
    ppermute x16 -> x0, waiting for transfers between devices: 22.8 us -> none  [the longest x14 22.8 us: from_behind(): return lax.ppermute(array, axis, pairs)]
    all_gather x1 -> x0, blocking collectives: 8.62 us -> none  [local(): lax.all_gather(near_src, 'rhs', axis=0, tiled=True)]
    gather x5 -> x0, local copies, waits for them, and re-layouts: 6.01 us -> none  [the longest x1 4.13 us: local(): jnp.take(gathered_all.reshape(vec_rows, senders * leaves_here, rank_dim),...]
  transfers between devices with their start and end apart: 18 -> 0, of which waited for: 10 -> 0; matrix products, arithmetic and copies ran while one was open for 21% -> 0% of each run, Pallas kernels for 0% -> 0%
where the time goes in v1:
time: 34.3 us; the launch traced here: 34.2 us
  Pallas kernels  32.6 us (95%)
  local copies, waits for them, and re-layouts  1.57 us (5%)
    pallas_call x1, Pallas kernels, local(): pl.pallas_call(functools.partial(kernel, n_leaf, n_rhs, plane), out_shape...  32.6 us
    unnamed x1, local copies, waits for them, and re-layouts  1.57 us

profile of v1, /device:TPU:1, one launch (start us, length us, event | category | flops | bytes accessed | tf_op | source)
XLA Modules:
  0.0 34.2 jit_solution(4050213271600033066)
XLA Ops:
  0.0 32.6 %hierarchical_product.1 = f32[16,2048]{1,0:T(8,128)} custom-call(bf16[16,2048]{1,0:T(8,128)(2,1)} %vectors.1, bf16[4,16,128,128]{3,2,1,0:T(8,128)(2,1)} %near_blocks.1, s32[4,16]{1,0:T(4,128)} %near_src.1, bf16[16,64,128]{2,1,0:T(8,128)(2,1)} %basis.1, bf16[15,64,128]{2,1,0:T(8,128)(2,1)} %local_transfer.1, bf16[16,64,384]{2,1,0:T(8,128)(2,1)} %leaf_coupling.1, ...), custom_call_target="tpu_custom_call" | custom-call | tf_op jit(solution)/shard_map/hierarchical_product/pallas_call | solution.py:449
  32.6 1.6 %copy.12 = f32[16,2048]{1,0:T(8,128)} copy(f32[16,2048]{1,0:T(8,128)} %hierarchical_product.1) | data formatting | bytes 262144

commit v2 on v1

--- a/solution.py
+++ b/solution.py
@@ -76,6 +76,7 @@
     recv_2,
     part_send,
     part_recv,
+    ready,
 ):
     vecs, span = vectors.shape
     leaves, rank, leaf_size = basis.shape
@@ -123,18 +124,24 @@
             barrier, inc=1, device_id=(leaf_index, rhs_index), device_id_type=MESH
         )
 
+    def loop(first, last, step):
+        def body(i, carry):
+            step(i)
+            return carry
+
+        lax.fori_loop(first, last, body, 0)
+
+    steps = range(1, 4)
     for k in range(1, n_rhs):
         greet(device, lax.rem(row + k, n_rhs))
-    for offset in offsets:
-        greet(leaf_at(offset), row)
     for k in range(1, plane):
         greet(in_plane(lax.rem(place + k, plane)), row)
-
-    def greet_column(k, carry):
-        greet(in_column(lax.rem(level + k, planes)), row)
-        return carry
-
-    lax.fori_loop(1, planes, greet_column, 0)
+    for k in steps:
+        greet(leaf_at(n_leaf - k), row)
+        pl.when(device + k < n_leaf)(functools.partial(greet, leaf_at(k), row))
+    loop(level + 1, planes, lambda other: greet(in_column(other), row))
+    behind = sum((device >= k).astype(jnp.int32) for k in steps)
+    greetings = (n_rhs - 1) + (plane - 1) + len(steps) + behind + level
 
     def send(src, dst, send_sem, recv_sem, leaf_index, rhs_index):
         pltpu.make_async_remote_copy(
@@ -149,53 +156,26 @@
     def wait_bytes(ref, sem):
         pltpu.make_async_copy(ref, ref, sem).wait()
 
+    lanes = lax.broadcasted_iota(jnp.int32, (vecs, 2 * rank), 1)
+    low = lanes < rank
+
+    def in_half(value, side):
+        return jnp.where((lanes >= rank) == (side == 1), value, 0.0).astype(BF16)
+
+    def both(product):
+        return jnp.where(low, product[:vecs], product[vecs:])
+
+    def pair_of(ref, node):
+        return ref[node : node + 2].reshape(2 * rank, -1)
+
     loads[0].wait()
     points = [own[:, t * leaf_size : (t + 1) * leaf_size] for t in range(leaves)]
-    for t in range(leaves):
-        mine[t] = points[t]
-        window[leaves + t, my_rows] = points[t]
-    pl.semaphore_wait(barrier, (n_rhs - 1) + len(offsets) + (plane - 1) + (planes - 1))
-
-    before, centre, after = (pl.ds(i * leaves, leaves) for i in range(3))
-    for k in range(1, n_rhs):
-        send(
-            mine,
-            window.at[centre, my_rows],
-            gather_send,
-            gather_recv.at[k - 1],
-            device,
-            lax.rem(row + k, n_rhs),
-        )
-    send(mine, window.at[before, my_rows], side_send.at[0], side_recv.at[0], leaf_at(1), row)
-    send(
-        mine, window.at[after, my_rows], side_send.at[1], side_recv.at[1], leaf_at(n_leaf - 1), row
-    )
-
-    lanes = lax.broadcasted_iota(jnp.int32, (vecs, 2 * rank), 1)
-    low = lanes < rank
-
-    def in_half(value, side):
-        return jnp.where((lanes >= rank) == (side == 1), value, 0.0).astype(BF16)
-
-    def both(product):
-        return jnp.where(low, product[:vecs], product[vecs:])
-
-    def pair_of(ref, node):
-        return ref[node : node + 2].reshape(2 * rank, -1)
-
     loads[1].wait()
-    pairs = []
+    ups = []
     for c in range(leaves // 2):
         rows = jnp.concatenate([points[2 * c], points[2 * c + 1]], axis=0)
-        pair = both(rows_by_rows(rows, pair_of(bases, 2 * c)))
-        turned = pltpu.roll(pair, rank, 1)
-        for leaf, value in (
-            (2 * c, jnp.where(low, pair, turned).astype(BF16)),
-            (2 * c + 1, jnp.where(low, turned, pair).astype(BF16)),
-        ):
-            leaf_up[leaf] = value
-            pool[leaf] = value
-        pairs.append(pair.astype(BF16))
+        ups.append(both(rows_by_rows(rows, pair_of(bases, 2 * c))))
+    pairs = [pair.astype(BF16) for pair in ups]
     loads[2].wait()
     start = 0
     while len(pairs) > 1:
@@ -236,7 +216,9 @@
             [shares[height - 1].astype(BF16), whole_share], axis=1
         )
     arrived_1[place] = message_1[0]
-    for height in range(1, plane_levels + 1):
+
+    pl.semaphore_wait(barrier, greetings)
+    for height in range(plane_levels, 0, -1):
         for i in range(1 << height - 1):
             send(
                 message_1.at[height - 1],
@@ -247,44 +229,101 @@
                 row,
             )
 
+    def tell(other):
+        pl.semaphore_signal(
+            ready, inc=1, device_id=(in_column(other), row), device_id_type=MESH
+        )
+
+    loop(0, level, tell)
+    for k in steps:
+
+        @pl.when(device + k >= n_leaf)
+        def _(k=k):
+            pl.semaphore_signal(
+                ready, inc=1, device_id=(leaf_at(k), row), device_id_type=MESH
+            )
+
+    for t in range(leaves):
+        mine[t] = points[t]
+        window[leaves + t, my_rows] = points[t]
+    before, centre, after = (pl.ds(i * leaves, leaves) for i in range(3))
+    for k in (2, 1, 3):
+        if k < n_rhs:
+            send(
+                mine,
+                window.at[centre, my_rows],
+                gather_send,
+                gather_recv.at[k - 1],
+                device,
+                lax.rem(row + k, n_rhs),
+            )
+
+    def to_neighbours(piece, rows):
+        @pl.when(device + 1 < n_leaf)
+        def _():
+            send(
+                piece, window.at[before, rows], side_send.at[0], side_recv.at[0], leaf_at(1), row
+            )
+
+        @pl.when(device > 0)
+        def _():
+            send(
+                piece,
+                window.at[after, rows],
+                side_send.at[1],
+                side_recv.at[1],
+                leaf_at(n_leaf - 1),
+                row,
+            )
+
+    to_neighbours(mine, my_rows)
+
+    for c, pair in enumerate(ups):
+        turned = pltpu.roll(pair, rank, 1)
+        for leaf, value in (
+            (2 * c, jnp.where(low, pair, turned).astype(BF16)),
+            (2 * c + 1, jnp.where(low, turned, pair).astype(BF16)),
+        ):
+            leaf_up[leaf] = value
+            pool[leaf] = value
+
+    def send_far(i):
+        send(
+            staged.at[i],
+            pool.at[leaves + device],
+            far_send,
+            far_recv,
+            leaf_at(offsets[i]),
+            row,
+        )
+
+    def far_goes_early(i):
+        offset = offsets[i]
+        if offset <= 3:
+            return None
+        return device >= n_leaf - offset
+
     for i, offset in enumerate(offsets):
         wants[i].wait()
         staged[i] = leaf_up[want_s[i, device]]
-        send(
-            staged.at[i], pool.at[leaves + device], far_send, far_recv, leaf_at(offset), row
-        )
-
-    for k in range(1, n_rhs):
-        theirs = pl.ds(pl.multiple_of(lax.rem(row + n_rhs - k, n_rhs) * vecs, vecs), vecs)
-        piece = window.at[centre, theirs]
-        wait_bytes(piece, gather_recv.at[k - 1])
-        send(piece, window.at[before, theirs], side_send.at[0], side_recv.at[0], leaf_at(1), row)
-        send(
-            piece,
-            window.at[after, theirs],
-            side_send.at[1],
-            side_recv.at[1],
-            leaf_at(n_leaf - 1),
-            row,
-        )
+        early = far_goes_early(i)
+        if early is None:
+            send_far(i)
+        else:
+            pl.when(early)(functools.partial(send_far, i))
 
     wait_bytes(arrived_1.at[pl.ds(0, plane - 1)], recv_1)
-    siblings = []
-    for height in range(1, plane_levels + 1):
-        first = sibling_start(place, height)
-        siblings.append(
-            sum(arrived_1[first + i].astype(F32)[:, : 2 * rank] for i in range(1 << height - 1))
-        )
     plane_up = sum(arrived_1[i].astype(F32)[:, 2 * rank :] for i in range(plane))
     share = plane_up
     for height in range(plane_levels + 1, top_levels + 1):
         if height > plane_levels + 1:
             share = lifted(share, height - 1)
         message_2[height - plane_levels - 1] = share.astype(BF16)
-    for height in range(1, column_levels + 1):
+
+    def send_column(height):
         first = sibling_start(level, height)
 
-        def send_column(i, carry, height=height, first=first):
+        def one(i):
             send(
                 message_2.at[height - 1],
                 arrived_2.at[level],
@@ -293,18 +332,95 @@
                 in_column(first + i),
                 row,
             )
-            return carry
-
-        lax.fori_loop(0, 1 << height - 1, send_column, 0)
-
-    wait_bytes(staged, far_recv)
+
+        loop(0, 1 << height - 1, one)
+
+    for height in range(column_levels, 0, -1):
+        pl.when(side_at(plane_levels + height) == 1)(functools.partial(send_column, height))
+
+    for k in (1, 3, 2):
+        if k < n_rhs:
+            theirs = pl.ds(pl.multiple_of(lax.rem(row + n_rhs - k, n_rhs) * vecs, vecs), vecs)
+            piece = window.at[centre, theirs]
+            wait_bytes(piece, gather_recv.at[k - 1])
+            to_neighbours(piece, theirs)
+
+    loads[8].wait()
+
+    def term(sibling, height):
+        return rows_by_rows(
+            in_half(sibling, side_at(height)), twice(top_couplings[height - 1])
+        )
+
+    terms = []
+    for height in range(1, plane_levels + 1):
+        first = sibling_start(place, height)
+        sibling = sum(
+            arrived_1[first + i].astype(F32)[:, : 2 * rank] for i in range(1 << height - 1)
+        )
+        terms.append(term(sibling, height))
+
+    above = planes - 1 - level + len(steps) - behind
+
+    @pl.when(above > 0)
+    def _():
+        pl.semaphore_wait(ready, above)
+
+    for height in range(column_levels, 0, -1):
+        pl.when(side_at(plane_levels + height) == 0)(functools.partial(send_column, height))
+    for i in range(len(offsets)):
+        early = far_goes_early(i)
+        if early is not None:
+            pl.when(jnp.logical_not(early))(functools.partial(send_far, i))
+
+    loads[5].wait()
+    loads[6].wait()
+
+    @pl.when(device > 0)
+    def _():
+        wait_bytes(window.at[before], side_recv.at[0])
+
+    @pl.when(device + 1 < n_leaf)
+    def _():
+        wait_bytes(window.at[after], side_recv.at[1])
+
+    slots = blocks.shape[0]
+    first_leaf = (device - 1) * leaves
+    width = NEAR_CHUNK * leaf_size
+    for chunk in range(leaves // NEAR_CHUNK):
+        for leaf in range(chunk * NEAR_CHUNK, (chunk + 1) * NEAR_CHUNK):
+            sources = jnp.concatenate(
+                [
+                    window[(src_s[q, leaf] - first_leaf) & (window.shape[0] - 1)]
+                    for q in range(slots)
+                ],
+                axis=1,
+            )
+            matrix = jnp.concatenate([blocks[q, leaf] for q in range(slots)], axis=1)
+            partial[:, leaf * leaf_size : (leaf + 1) * leaf_size] = rows_by_rows(
+                sources, matrix
+            ).astype(BF16)
+        cols = pl.ds(chunk * width, width)
+        for k in (2, 1, 3):
+            if k < n_rhs:
+                target = lax.rem(row + k, n_rhs)
+                theirs = pl.ds(pl.multiple_of(target * vecs, vecs), vecs)
+                send(
+                    partial.at[theirs, cols],
+                    others.at[k - 1, :, cols],
+                    part_send,
+                    part_recv,
+                    device,
+                    target,
+                )
+
     loads[4].wait()
     loads[7].wait()
+    wait_bytes(staged, far_recv)
+    far = couplings.shape[2] // rank
 
     def far_block(leaf, f):
         return pool[far_s[f, leaf]].astype(F32)
-
-    far = couplings.shape[2] // rank
 
     def far_row(leaf):
         return jnp.concatenate(
@@ -319,47 +435,19 @@
         sources = jnp.concatenate([far_row(2 * c), far_row(2 * c + 1)], axis=0)
         coupled[c] = both(rows_by_rows(sources, pair_of(couplings, 2 * c)))
 
-    loads[5].wait()
-    loads[6].wait()
-    wait_bytes(window.at[before], side_recv.at[0])
-    wait_bytes(window.at[after], side_recv.at[1])
-    slots = blocks.shape[0]
-    first_leaf = (device - 1) * leaves
-    width = NEAR_CHUNK * leaf_size
-    for chunk in range(leaves // NEAR_CHUNK):
-        for leaf in range(chunk * NEAR_CHUNK, (chunk + 1) * NEAR_CHUNK):
-            sources = jnp.concatenate(
-                [
-                    window[(src_s[q, leaf] - first_leaf) & (window.shape[0] - 1)] for q in range(slots)
-                ],
-                axis=1,
-            )
-            matrix = jnp.concatenate([blocks[q, leaf] for q in range(slots)], axis=1)
-            partial[:, leaf * leaf_size : (leaf + 1) * leaf_size] = rows_by_rows(
-                sources, matrix
-            ).astype(BF16)
-        cols = pl.ds(chunk * width, width)
-        for k in range(1, n_rhs):
-            target = lax.rem(row + k, n_rhs)
-            theirs = pl.ds(pl.multiple_of(target * vecs, vecs), vecs)
-            send(
-                partial.at[theirs, cols],
-                others.at[k - 1, :, cols],
-                part_send,
-                part_recv,
-                device,
-                target,
-            )
+    wait_bytes(others, part_recv)
+    for leaf in range(leaves):
+        cols = slice(leaf * leaf_size, (leaf + 1) * leaf_size)
+        total = partial[my_rows, cols].astype(F32)
+        for k in range(n_rhs - 1):
+            total = total + others[k, :, cols].astype(F32)
+        out[:, cols] = total
 
     wait_bytes(arrived_2.at[pl.ds(0, planes - 1)], recv_2)
     for height in range(1, column_levels + 1):
         first = sibling_start(level, height)
-        siblings.append(sum(arrived_2[first + i].astype(F32) for i in range(1 << height - 1)))
-    loads[8].wait()
-    terms = [
-        rows_by_rows(in_half(siblings[height - 1], side_at(height)), twice(top_couplings[height - 1]))
-        for height in range(1, top_levels + 1)
-    ]
+        sibling = sum(arrived_2[first + i].astype(F32) for i in range(1 << height - 1))
+        terms.append(term(sibling, plane_levels + height))
     down = in_half(terms[top_levels - 1], side_at(top_levels))
     for height in range(top_levels - 1, 0, -1):
         spread = rows_by_cols(down, twice(top_moves[height - 1]))
@@ -379,21 +467,24 @@
         ]
         pairs = [half for both_now in spreads for half in (both_now[:vecs], both_now[vecs:])]
 
-    wait_bytes(others, part_recv)
     for c, pair in enumerate(pairs):
         far_part = rows_by_cols(split(pair + coupled[c]), pair_of(bases, 2 * c))
         for leaf, value in ((2 * c, far_part[:vecs]), (2 * c + 1, far_part[vecs:])):
             cols = slice(leaf * leaf_size, (leaf + 1) * leaf_size)
-            total = value + partial[my_rows, cols].astype(F32)
-            for k in range(n_rhs - 1):
-                total = total + others[k, :, cols].astype(F32)
-            out[:, cols] = total
+            out[:, cols] = out[:, cols] + value
 
     if n_rhs > 1:
         wait_bytes(others, gather_send)
         wait_bytes(others, part_send)
-    wait_bytes(window.at[before], side_send.at[0])
-    wait_bytes(window.at[after], side_send.at[1])
+
+    @pl.when(device + 1 < n_leaf)
+    def _():
+        wait_bytes(window.at[before], side_send.at[0])
+
+    @pl.when(device > 0)
+    def _():
+        wait_bytes(window.at[after], side_send.at[1])
+
     wait_bytes(staged, far_send)
     wait_bytes(arrived_1.at[pl.ds(0, plane - 1)], send_1)
     wait_bytes(arrived_2.at[pl.ds(0, planes - 1)], send_2)
@@ -445,10 +536,11 @@
         dma,
         dma,
         dma,
+        pltpu.SemaphoreType.REGULAR,
     ]
     return pl.pallas_call(
         functools.partial(kernel, n_leaf, n_rhs, plane),
-        out_shape=jax.ShapeDtypeStruct((vecs, span), F32),
+        out_shape=pltpu.VMEM((vecs, span), F32),
         in_specs=[pl.BlockSpec(memory_space=pltpu.HBM)] * 10,
         out_specs=pl.BlockSpec(memory_space=pltpu.VMEM),
         scratch_shapes=scratch,

time: 34.3 us -> 28.3 us (0.83)
  Pallas kernels: 32.6 us -> 27.5 us
  local copies, waits for them, and re-layouts: 1.57 us -> 0.66 us
    pallas_call x1, Pallas kernels: 32.6 us -> 27.5 us  [local(): pl.pallas_call(functools.partial(kernel, n_leaf, n_rhs, plane), out_shape...]
    unnamed x1, local copies, waits for them, and re-layouts: 1.57 us -> 0.66 us
where the time goes in v2:
time: 28.3 us; the launch traced here: 28.2 us
  Pallas kernels  27.5 us (97%)
  local copies, waits for them, and re-layouts  0.66 us (2%)
    pallas_call x1, Pallas kernels, local(): pl.pallas_call(functools.partial(kernel, n_leaf, n_rhs, plane), out_shape...  27.5 us
    unnamed x1, local copies, waits for them, and re-layouts  0.66 us

profile of v2, /device:TPU:1, one launch (start us, length us, event | category | flops | bytes accessed | tf_op | source)
XLA Modules:
  0.0 28.2 jit_solution(11550053940333088681)
XLA Ops:
  0.0 27.5 %hierarchical_product.1 = f32[16,2048]{1,0:T(8,128)S(1)} custom-call(bf16[16,2048]{1,0:T(8,128)(2,1)} %vectors.1, bf16[4,16,128,128]{3,2,1,0:T(8,128)(2,1)} %near_blocks.1, s32[4,16]{1,0:T(4,128)} %near_src.1, bf16[16,64,128]{2,1,0:T(8,128)(2,1)} %basis.1, bf16[15,64,128]{2,1,0:T(8,128)(2,1)} %local_transfer.1, bf16[16,64,384]{2,1,0:T(8,128)(2,1)} %leaf_coupling.1, ...), custom_call_target="tpu_custom_call" | custom-call | tf_op jit(solution)/shard_map/hierarchical_product/pallas_call | solution.py:541
  27.5 0.7 %copy.12 = f32[16,2048]{1,0:T(8,128)} copy(f32[16,2048]{1,0:T(8,128)S(1)} %hierarchical_product.1) | data formatting | bytes 262144

commit v3 on v2

--- a/solution.py
+++ b/solution.py
@@ -60,6 +60,7 @@
     message_2,
     arrived_2,
     coupled,
+    wide,
     partial,
     others,
     load_sem,
@@ -159,8 +160,11 @@
     lanes = lax.broadcasted_iota(jnp.int32, (vecs, 2 * rank), 1)
     low = lanes < rank
 
+    def high_lanes(value):
+        return lax.broadcasted_iota(jnp.int32, value.shape, 1) >= rank
+
     def in_half(value, side):
-        return jnp.where((lanes >= rank) == (side == 1), value, 0.0).astype(BF16)
+        return jnp.where(high_lanes(value) == (side == 1), value, 0.0).astype(BF16)
 
     def both(product):
         return jnp.where(low, product[:vecs], product[vecs:])
@@ -352,26 +356,60 @@
             in_half(sibling, side_at(height)), twice(top_couplings[height - 1])
         )
 
-    terms = []
-    for height in range(1, plane_levels + 1):
-        first = sibling_start(place, height)
-        sibling = sum(
-            arrived_1[first + i].astype(F32)[:, : 2 * rank] for i in range(1 << height - 1)
-        )
-        terms.append(term(sibling, height))
+    def split(pair):
+        high = high_lanes(pair)
+        return jnp.concatenate(
+            [jnp.where(high, 0.0, pair), jnp.where(high, pair, 0.0)], axis=0
+        ).astype(BF16)
+
+    unit_rows = lax.broadcasted_iota(jnp.int32, (rank, 2 * rank), 0)
+    unit_lanes = lax.broadcasted_iota(jnp.int32, (rank, 2 * rank), 1)
+    unit = jnp.where((unit_lanes == unit_rows) | (unit_lanes == unit_rows + rank), 1.0, 0.0)
+    down = in_half(term(unit, top_levels), side_at(top_levels))
+    for height in range(top_levels - 1, 0, -1):
+        spread = rows_by_cols(down, twice(top_moves[height - 1]))
+        if height > plane_levels:
+            spread = jnp.concatenate([term(unit, height), spread], axis=0)
+        else:
+            first = sibling_start(place, height)
+            sibling = sum(
+                arrived_1[first + i].astype(F32)[:, : 2 * rank] for i in range(1 << height - 1)
+            )
+            own_term = term(sibling, height)
+            if height == plane_levels:
+                spread = jnp.concatenate([own_term, spread], axis=0)
+            else:
+                spread = jnp.concatenate([spread[:vecs] + own_term, spread[vecs:]], axis=0)
+        down = in_half(spread, side_at(height))
+    pairs = [rows_by_cols(down, twice(moves[start]))]
+    rows_now = pairs[0].shape[0]
+    while len(pairs) < leaves // 2:
+        start -= 2 * len(pairs)
+        spreads = [
+            rows_by_cols(split(pair), pair_of(moves, start + 2 * c))
+            for c, pair in enumerate(pairs)
+        ]
+        pairs = [half for both_now in spreads for half in (both_now[:rows_now], both_now[rows_now:])]
+    for c, pair in enumerate(pairs):
+        coupled[c] = pair[:vecs]
+        wide[c] = pair[vecs:].astype(BF16)
 
     above = planes - 1 - level + len(steps) - behind
 
-    @pl.when(above > 0)
-    def _():
-        pl.semaphore_wait(ready, above)
-
-    for height in range(column_levels, 0, -1):
-        pl.when(side_at(plane_levels + height) == 0)(functools.partial(send_column, height))
-    for i in range(len(offsets)):
-        early = far_goes_early(i)
-        if early is not None:
-            pl.when(jnp.logical_not(early))(functools.partial(send_far, i))
+    def send_above():
+        @pl.when(above > 0)
+        def _():
+            pl.semaphore_wait(ready, above)
+
+        for height in range(column_levels, 0, -1):
+            pl.when(side_at(plane_levels + height) == 0)(functools.partial(send_column, height))
+        for i in range(len(offsets)):
+            early = far_goes_early(i)
+            if early is not None:
+                pl.when(jnp.logical_not(early))(functools.partial(send_far, i))
+
+    upper_half = level >= planes // 2
+    pl.when(upper_half)(send_above)
 
     loads[5].wait()
     loads[6].wait()
@@ -414,6 +452,8 @@
                     target,
                 )
 
+    pl.when(jnp.logical_not(upper_half))(send_above)
+
     loads[4].wait()
     loads[7].wait()
     wait_bytes(staged, far_recv)
@@ -433,45 +473,36 @@
 
     for c in range(leaves // 2):
         sources = jnp.concatenate([far_row(2 * c), far_row(2 * c + 1)], axis=0)
-        coupled[c] = both(rows_by_rows(sources, pair_of(couplings, 2 * c)))
-
-    wait_bytes(others, part_recv)
-    for leaf in range(leaves):
-        cols = slice(leaf * leaf_size, (leaf + 1) * leaf_size)
-        total = partial[my_rows, cols].astype(F32)
-        for k in range(n_rhs - 1):
-            total = total + others[k, :, cols].astype(F32)
-        out[:, cols] = total
+        coupled[c] = coupled[c] + both(rows_by_rows(sources, pair_of(couplings, 2 * c)))
+
+    def add_near():
+        wait_bytes(others, part_recv)
+        for leaf in range(leaves):
+            cols = slice(leaf * leaf_size, (leaf + 1) * leaf_size)
+            total = out[:, cols] + partial[my_rows, cols].astype(F32)
+            for k in range(n_rhs - 1):
+                total = total + others[k, :, cols].astype(F32)
+            out[:, cols] = total
+
+    out[...] = jnp.zeros_like(out)
+    pl.when(jnp.logical_not(upper_half))(add_near)
 
     wait_bytes(arrived_2.at[pl.ds(0, planes - 1)], recv_2)
+    siblings = []
     for height in range(1, column_levels + 1):
         first = sibling_start(level, height)
-        sibling = sum(arrived_2[first + i].astype(F32) for i in range(1 << height - 1))
-        terms.append(term(sibling, plane_levels + height))
-    down = in_half(terms[top_levels - 1], side_at(top_levels))
-    for height in range(top_levels - 1, 0, -1):
-        spread = rows_by_cols(down, twice(top_moves[height - 1]))
-        down = in_half(terms[height - 1] + spread, side_at(height))
-
-    def split(pair):
-        return jnp.concatenate(
-            [jnp.where(low, pair, 0.0), jnp.where(low, 0.0, pair)], axis=0
-        ).astype(BF16)
-
-    pairs = [rows_by_cols(down, twice(moves[start]))]
-    while len(pairs) < leaves // 2:
-        start -= 2 * len(pairs)
-        spreads = [
-            rows_by_cols(split(pair), pair_of(moves, start + 2 * c))
-            for c, pair in enumerate(pairs)
-        ]
-        pairs = [half for both_now in spreads for half in (both_now[:vecs], both_now[vecs:])]
-
-    for c, pair in enumerate(pairs):
-        far_part = rows_by_cols(split(pair + coupled[c]), pair_of(bases, 2 * c))
+        siblings.append(sum(arrived_2[first + i].astype(F32) for i in range(1 << height - 1)))
+    siblings = jnp.concatenate(
+        [jnp.where(low, *siblings[i : i + 2]) for i in range(0, column_levels, 2)], axis=1
+    ).astype(BF16)
+    for c in range(leaves // 2):
+        pair = coupled[c] + rows_by_cols(siblings, wide[c])
+        far_part = rows_by_cols(split(pair), pair_of(bases, 2 * c))
         for leaf, value in ((2 * c, far_part[:vecs]), (2 * c + 1, far_part[vecs:])):
             cols = slice(leaf * leaf_size, (leaf + 1) * leaf_size)
             out[:, cols] = out[:, cols] + value
+
+    pl.when(upper_half)(add_near)
 
     if n_rhs > 1:
         wait_bytes(others, gather_send)
@@ -520,6 +551,7 @@
         pltpu.VMEM((levels[1], vecs, 2 * rank), BF16),
         pltpu.VMEM((planes, vecs, 2 * rank), BF16),
         pltpu.VMEM((leaves // 2, vecs, 2 * rank), F32),
+        pltpu.VMEM((leaves // 2, levels[1] * rank, 2 * rank), BF16),
         pltpu.VMEM((n_rhs * vecs, span), BF16),
         pltpu.VMEM((max(n_rhs - 1, 1), vecs, span), BF16),
         dma((9,)),

time: 28.3 us -> 26.9 us (0.951)
  Pallas kernels: 27.5 us -> 26.1 us
    pallas_call x1, Pallas kernels: 27.5 us -> 26.1 us  [local(): pl.pallas_call(functools.partial(kernel, n_leaf, n_rhs, plane), out_shape...]
where the time goes in v3:
time: 26.9 us; the launch traced here: 26.8 us
  Pallas kernels  26.1 us (97%)
  local copies, waits for them, and re-layouts  0.66 us (2%)
    pallas_call x1, Pallas kernels, local(): pl.pallas_call(functools.partial(kernel, n_leaf, n_rhs, plane), out_shape...  26.1 us
    unnamed x1, local copies, waits for them, and re-layouts  0.66 us

profile of v3, /device:TPU:1, one launch (start us, length us, event | category | flops | bytes accessed | tf_op | source)
XLA Modules:
  0.0 26.8 jit_solution(4829445228615360198)
XLA Ops:
  0.0 26.1 %hierarchical_product.1 = f32[16,2048]{1,0:T(8,128)S(1)} custom-call(bf16[16,2048]{1,0:T(8,128)(2,1)} %vectors.1, bf16[4,16,128,128]{3,2,1,0:T(8,128)(2,1)} %near_blocks.1, s32[4,16]{1,0:T(4,128)} %near_src.1, bf16[16,64,128]{2,1,0:T(8,128)(2,1)} %basis.1, bf16[15,64,128]{2,1,0:T(8,128)(2,1)} %local_transfer.1, bf16[16,64,384]{2,1,0:T(8,128)(2,1)} %leaf_coupling.1, ...), custom_call_target="tpu_custom_call" | custom-call | tf_op jit(solution)/shard_map/hierarchical_product/pallas_call | solution.py:573
  26.1 0.7 %copy.12 = f32[16,2048]{1,0:T(8,128)} copy(f32[16,2048]{1,0:T(8,128)S(1)} %hierarchical_product.1) | data formatting | bytes 262144

commit v4 on v3

--- a/solution.py
+++ b/solution.py
@@ -115,7 +115,7 @@
         )
         for i, offset in enumerate(offsets)
     ]
-    for load in loads + wants:
+    for load in loads[:4]:
         load.start()
 
     barrier = pltpu.get_barrier_semaphore()
@@ -174,6 +174,50 @@
 
     loads[0].wait()
     points = [own[:, t * leaf_size : (t + 1) * leaf_size] for t in range(leaves)]
+    before, centre, after = (pl.ds(i * leaves, leaves) for i in range(3))
+
+    def to_neighbours(piece, rows):
+        @pl.when(device + 1 < n_leaf)
+        def _():
+            send(
+                piece, window.at[before, rows], side_send.at[0], side_recv.at[0], leaf_at(1), row
+            )
+
+        @pl.when(device > 0)
+        def _():
+            send(
+                piece,
+                window.at[after, rows],
+                side_send.at[1],
+                side_recv.at[1],
+                leaf_at(n_leaf - 1),
+                row,
+            )
+
+    def spread_points():
+        for t in range(leaves):
+            mine[t] = points[t]
+            window[leaves + t, my_rows] = points[t]
+        for k in (2, 1, 3):
+            if k < n_rhs:
+                send(
+                    mine,
+                    window.at[centre, my_rows],
+                    gather_send,
+                    gather_recv.at[k - 1],
+                    device,
+                    lax.rem(row + k, n_rhs),
+                )
+
+        to_neighbours(mine, my_rows)
+
+    upper_half = level >= planes // 2
+
+    @pl.when(jnp.logical_not(upper_half))
+    def _():
+        pl.semaphore_wait(barrier, greetings)
+        spread_points()
+
     loads[1].wait()
     ups = []
     for c in range(leaves // 2):
@@ -221,7 +265,10 @@
         )
     arrived_1[place] = message_1[0]
 
-    pl.semaphore_wait(barrier, greetings)
+    @pl.when(upper_half)
+    def _():
+        pl.semaphore_wait(barrier, greetings)
+
     for height in range(plane_levels, 0, -1):
         for i in range(1 << height - 1):
             send(
@@ -247,40 +294,10 @@
                 ready, inc=1, device_id=(leaf_at(k), row), device_id_type=MESH
             )
 
-    for t in range(leaves):
-        mine[t] = points[t]
-        window[leaves + t, my_rows] = points[t]
-    before, centre, after = (pl.ds(i * leaves, leaves) for i in range(3))
-    for k in (2, 1, 3):
-        if k < n_rhs:
-            send(
-                mine,
-                window.at[centre, my_rows],
-                gather_send,
-                gather_recv.at[k - 1],
-                device,
-                lax.rem(row + k, n_rhs),
-            )
-
-    def to_neighbours(piece, rows):
-        @pl.when(device + 1 < n_leaf)
-        def _():
-            send(
-                piece, window.at[before, rows], side_send.at[0], side_recv.at[0], leaf_at(1), row
-            )
-
-        @pl.when(device > 0)
-        def _():
-            send(
-                piece,
-                window.at[after, rows],
-                side_send.at[1],
-                side_recv.at[1],
-                leaf_at(n_leaf - 1),
-                row,
-            )
-
-    to_neighbours(mine, my_rows)
+    for load in wants + loads[4:]:
+        load.start()
+
+    pl.when(upper_half)(spread_points)
 
     for c, pair in enumerate(ups):
         turned = pltpu.roll(pair, rank, 1)
@@ -316,13 +333,19 @@
         else:
             pl.when(early)(functools.partial(send_far, i))
 
+    unit_rows = lax.broadcasted_iota(jnp.int32, (rank, 2 * rank), 0)
+    unit_lanes = lax.broadcasted_iota(jnp.int32, (rank, 2 * rank), 1)
+    unit = jnp.where((unit_lanes == unit_rows) | (unit_lanes == unit_rows + rank), 1.0, 0.0)
+    lifts = [unit]
+    for height in range(plane_levels + 1, top_levels):
+        lifts.append(lifted(lifts[-1], height))
+    lift = jnp.concatenate([each.astype(BF16) for each in lifts[1:]], axis=1)
     wait_bytes(arrived_1.at[pl.ds(0, plane - 1)], recv_1)
-    plane_up = sum(arrived_1[i].astype(F32)[:, 2 * rank :] for i in range(plane))
-    share = plane_up
-    for height in range(plane_levels + 1, top_levels + 1):
-        if height > plane_levels + 1:
-            share = lifted(share, height - 1)
-        message_2[height - plane_levels - 1] = share.astype(BF16)
+    plane_up = sum(arrived_1[i].astype(F32)[:, 2 * rank :] for i in range(plane)).astype(BF16)
+    message_2[0] = plane_up
+    above_plane = rows_by_cols(plane_up[:, :rank], lift).astype(BF16)
+    for i in range(1, column_levels):
+        message_2[i] = above_plane[:, (i - 1) * 2 * rank : i * 2 * rank]
 
     def send_column(height):
         first = sibling_start(level, height)
@@ -362,9 +385,6 @@
             [jnp.where(high, 0.0, pair), jnp.where(high, pair, 0.0)], axis=0
         ).astype(BF16)
 
-    unit_rows = lax.broadcasted_iota(jnp.int32, (rank, 2 * rank), 0)
-    unit_lanes = lax.broadcasted_iota(jnp.int32, (rank, 2 * rank), 1)
-    unit = jnp.where((unit_lanes == unit_rows) | (unit_lanes == unit_rows + rank), 1.0, 0.0)
     down = in_half(term(unit, top_levels), side_at(top_levels))
     for height in range(top_levels - 1, 0, -1):
         spread = rows_by_cols(down, twice(top_moves[height - 1]))
@@ -408,8 +428,8 @@
             if early is not None:
                 pl.when(jnp.logical_not(early))(functools.partial(send_far, i))
 
-    upper_half = level >= planes // 2
-    pl.when(upper_half)(send_above)
+    early_planes = level < planes // 4
+    pl.when(jnp.logical_not(early_planes))(send_above)
 
     loads[5].wait()
     loads[6].wait()
@@ -452,7 +472,7 @@
                     target,
                 )
 
-    pl.when(jnp.logical_not(upper_half))(send_above)
+    pl.when(early_planes)(send_above)
 
     loads[4].wait()
     loads[7].wait()

time: 26.9 us -> 26.5 us (0.985)
  Pallas kernels: 26.1 us -> 25.7 us
    pallas_call x1, Pallas kernels: 26.1 us -> 25.7 us  [local(): pl.pallas_call(functools.partial(kernel, n_leaf, n_rhs, plane), out_shape...]
where the time goes in v4:
time: 26.5 us; the launch traced here: 26.4 us
  Pallas kernels  25.7 us (97%)
  local copies, waits for them, and re-layouts  0.66 us (2%)
    pallas_call x1, Pallas kernels, local(): pl.pallas_call(functools.partial(kernel, n_leaf, n_rhs, plane), out_shape...  25.7 us
    unnamed x1, local copies, waits for them, and re-layouts  0.66 us

profile of v4, /device:TPU:1, one launch (start us, length us, event | category | flops | bytes accessed | tf_op | source)
XLA Modules:
  0.0 26.4 jit_solution(132770701332936299)
XLA Ops:
  0.0 25.7 %hierarchical_product.1 = f32[16,2048]{1,0:T(8,128)S(1)} custom-call(bf16[16,2048]{1,0:T(8,128)(2,1)} %vectors.1, bf16[4,16,128,128]{3,2,1,0:T(8,128)(2,1)} %near_blocks.1, s32[4,16]{1,0:T(4,128)} %near_src.1, bf16[16,64,128]{2,1,0:T(8,128)(2,1)} %basis.1, bf16[15,64,128]{2,1,0:T(8,128)(2,1)} %local_transfer.1, bf16[16,64,384]{2,1,0:T(8,128)(2,1)} %leaf_coupling.1, ...), custom_call_target="tpu_custom_call" | custom-call | tf_op jit(solution)/shard_map/hierarchical_product/pallas_call | solution.py:593
  25.7 0.7 %copy.12 = f32[16,2048]{1,0:T(8,128)} copy(f32[16,2048]{1,0:T(8,128)S(1)} %hierarchical_product.1) | data formatting | bytes 262144

commit v5 on v4

--- a/solution.py
+++ b/solution.py
@@ -78,6 +78,7 @@
     part_send,
     part_recv,
     ready,
+    row_ready,
 ):
     vecs, span = vectors.shape
     leaves, rank, leaf_size = basis.shape
@@ -133,16 +134,16 @@
         lax.fori_loop(first, last, body, 0)
 
     steps = range(1, 4)
-    for k in range(1, n_rhs):
-        greet(device, lax.rem(row + k, n_rhs))
     for k in range(1, plane):
         greet(in_plane(lax.rem(place + k, plane)), row)
+    for k in range(1, n_rhs):
+        pl.when(row + k < n_rhs)(functools.partial(greet, device, row + k))
     for k in steps:
         greet(leaf_at(n_leaf - k), row)
         pl.when(device + k < n_leaf)(functools.partial(greet, leaf_at(k), row))
     loop(level + 1, planes, lambda other: greet(in_column(other), row))
     behind = sum((device >= k).astype(jnp.int32) for k in steps)
-    greetings = (n_rhs - 1) + (plane - 1) + len(steps) + behind + level
+    greetings = row + (plane - 1) + len(steps) + behind + level
 
     def send(src, dst, send_sem, recv_sem, leaf_index, rhs_index):
         pltpu.make_async_remote_copy(
@@ -194,29 +195,49 @@
                 row,
             )
 
-    def spread_points():
+    def send_points(k):
+        send(
+            mine,
+            window.at[centre, my_rows],
+            gather_send,
+            gather_recv.at[k - 1],
+            device,
+            lax.rem(row + k, n_rhs),
+        )
+
+    def tell_rows():
+        for k in range(1, n_rhs):
+
+            @pl.when(row >= k)
+            def _(k=k):
+                pl.semaphore_signal(
+                    row_ready, inc=1, device_id=(device, row - k), device_id_type=MESH
+                )
+
+    def points_below():
         for t in range(leaves):
             mine[t] = points[t]
             window[leaves + t, my_rows] = points[t]
-        for k in (2, 1, 3):
-            if k < n_rhs:
-                send(
-                    mine,
-                    window.at[centre, my_rows],
-                    gather_send,
-                    gather_recv.at[k - 1],
-                    device,
-                    lax.rem(row + k, n_rhs),
-                )
-
+        for k in range(1, n_rhs):
+            pl.when(row + k >= n_rhs)(functools.partial(send_points, k))
         to_neighbours(mine, my_rows)
 
+    def points_above():
+        @pl.when(row < n_rhs - 1)
+        def _():
+            pl.semaphore_wait(row_ready, n_rhs - 1 - row)
+            for k in range(1, n_rhs):
+                pl.when(row + k < n_rhs)(functools.partial(send_points, k))
+
     upper_half = level >= planes // 2
-
-    @pl.when(jnp.logical_not(upper_half))
+    early_planes = level < planes // 4
+
+    @pl.when(early_planes)
     def _():
         pl.semaphore_wait(barrier, greetings)
-        spread_points()
+        tell_rows()
+        points_below()
+        points_above()
 
     loads[1].wait()
     ups = []
@@ -258,16 +279,14 @@
     shares = [root]
     for height in range(1, plane_levels + 1):
         shares.append(lifted(shares[-1], height))
-    whole_share = shares[plane_levels].astype(BF16)
     for height in range(1, plane_levels + 1):
-        message_1[height - 1] = jnp.concatenate(
-            [shares[height - 1].astype(BF16), whole_share], axis=1
-        )
+        message_1[height - 1] = jnp.where(low, shares[height - 1], shares[plane_levels]).astype(BF16)
     arrived_1[place] = message_1[0]
 
-    @pl.when(upper_half)
+    @pl.when(jnp.logical_not(early_planes))
     def _():
         pl.semaphore_wait(barrier, greetings)
+        tell_rows()
 
     for height in range(plane_levels, 0, -1):
         for i in range(1 << height - 1):
@@ -297,7 +316,9 @@
     for load in wants + loads[4:]:
         load.start()
 
-    pl.when(upper_half)(spread_points)
+    @pl.when(jnp.logical_not(early_planes))
+    def _():
+        points_below()
 
     for c, pair in enumerate(ups):
         turned = pltpu.roll(pair, rank, 1)
@@ -333,19 +354,20 @@
         else:
             pl.when(early)(functools.partial(send_far, i))
 
+    pl.when(jnp.logical_not(early_planes))(points_above)
+
     unit_rows = lax.broadcasted_iota(jnp.int32, (rank, 2 * rank), 0)
     unit_lanes = lax.broadcasted_iota(jnp.int32, (rank, 2 * rank), 1)
     unit = jnp.where((unit_lanes == unit_rows) | (unit_lanes == unit_rows + rank), 1.0, 0.0)
     lifts = [unit]
     for height in range(plane_levels + 1, top_levels):
         lifts.append(lifted(lifts[-1], height))
-    lift = jnp.concatenate([each.astype(BF16) for each in lifts[1:]], axis=1)
+    lift = twice(jnp.concatenate([each.astype(BF16) for each in lifts], axis=1))
     wait_bytes(arrived_1.at[pl.ds(0, plane - 1)], recv_1)
-    plane_up = sum(arrived_1[i].astype(F32)[:, 2 * rank :] for i in range(plane)).astype(BF16)
-    message_2[0] = plane_up
-    above_plane = rows_by_cols(plane_up[:, :rank], lift).astype(BF16)
-    for i in range(1, column_levels):
-        message_2[i] = above_plane[:, (i - 1) * 2 * rank : i * 2 * rank]
+    plane_up = in_half(sum(arrived_1[i].astype(F32) for i in range(plane)), 1)
+    above_plane = rows_by_cols(plane_up, lift).astype(BF16)
+    for i in range(column_levels):
+        message_2[i] = above_plane[:, i * 2 * rank : (i + 1) * 2 * rank]
 
     def send_column(height):
         first = sibling_start(level, height)
@@ -360,7 +382,13 @@
                 row,
             )
 
-        loop(0, 1 << height - 1, one)
+        width = 1 << height - 1
+
+        def in_turn(i):
+            aside = lax.div(i + 1, 2) * (2 * lax.rem(i, 2) - 1)
+            one(lax.rem(lax.rem(level, width) + aside + width, width))
+
+        loop(0, width, in_turn)
 
     for height in range(column_levels, 0, -1):
         pl.when(side_at(plane_levels + height) == 1)(functools.partial(send_column, height))
@@ -392,9 +420,8 @@
             spread = jnp.concatenate([term(unit, height), spread], axis=0)
         else:
             first = sibling_start(place, height)
-            sibling = sum(
-                arrived_1[first + i].astype(F32)[:, : 2 * rank] for i in range(1 << height - 1)
-            )
+            sibling = sum(arrived_1[first + i].astype(F32) for i in range(1 << height - 1))
+            sibling = rows_by_cols(in_half(sibling, 0), twice(unit.astype(BF16)))
             own_term = term(sibling, height)
             if height == plane_levels:
                 spread = jnp.concatenate([own_term, spread], axis=0)
@@ -428,7 +455,6 @@
             if early is not None:
                 pl.when(jnp.logical_not(early))(functools.partial(send_far, i))
 
-    early_planes = level < planes // 4
     pl.when(jnp.logical_not(early_planes))(send_above)
 
     loads[5].wait()
@@ -566,8 +592,8 @@
         pltpu.VMEM((leaves, vecs, 2 * rank), BF16),
         pltpu.VMEM((leaves + n_leaf, vecs, 2 * rank), BF16),
         pltpu.VMEM((7, vecs, 2 * rank), BF16),
-        pltpu.VMEM((levels[0], vecs, 4 * rank), BF16),
-        pltpu.VMEM((plane, vecs, 4 * rank), BF16),
+        pltpu.VMEM((levels[0], vecs, 2 * rank), BF16),
+        pltpu.VMEM((plane, vecs, 2 * rank), BF16),
         pltpu.VMEM((levels[1], vecs, 2 * rank), BF16),
         pltpu.VMEM((planes, vecs, 2 * rank), BF16),
         pltpu.VMEM((leaves // 2, vecs, 2 * rank), F32),
@@ -588,6 +614,7 @@
         dma,
         dma,
         dma,
+        pltpu.SemaphoreType.REGULAR,
         pltpu.SemaphoreType.REGULAR,
     ]
     return pl.pallas_call(

time: 26.5 us -> 25.8 us (0.974)
  Pallas kernels: 25.7 us -> 24.8 us
    pallas_call x1, Pallas kernels: 25.7 us -> 24.8 us  [local(): pl.pallas_call(functools.partial(kernel, n_leaf, n_rhs, plane), out_shape...]
where the time goes in v5:
time: 25.8 us; the launch traced here: 25.5 us
  Pallas kernels  24.8 us (96%)
  local copies, waits for them, and re-layouts  0.66 us (3%)
    pallas_call x1, Pallas kernels, local(): pl.pallas_call(functools.partial(kernel, n_leaf, n_rhs, plane), out_shape...  24.8 us
    unnamed x1, local copies, waits for them, and re-layouts  0.66 us

profile of v5, /device:TPU:1, one launch (start us, length us, event | category | flops | bytes accessed | tf_op | source)
XLA Modules:
  0.0 25.5 jit_solution(3489843920079173303)
XLA Ops:
  0.0 24.8 %hierarchical_product.1 = f32[16,2048]{1,0:T(8,128)S(1)} custom-call(bf16[16,2048]{1,0:T(8,128)(2,1)} %vectors.1, bf16[4,16,128,128]{3,2,1,0:T(8,128)(2,1)} %near_blocks.1, s32[4,16]{1,0:T(4,128)} %near_src.1, bf16[16,64,128]{2,1,0:T(8,128)(2,1)} %basis.1, bf16[15,64,128]{2,1,0:T(8,128)(2,1)} %local_transfer.1, bf16[16,64,384]{2,1,0:T(8,128)(2,1)} %leaf_coupling.1, ...), custom_call_target="tpu_custom_call" | custom-call | tf_op jit(solution)/shard_map/hierarchical_product/pallas_call | solution.py:620
  24.8 0.7 %copy.12 = f32[16,2048]{1,0:T(8,128)} copy(f32[16,2048]{1,0:T(8,128)S(1)} %hierarchical_product.1) | data formatting | bytes 262144

commit v6 on v5

--- a/solution.py
+++ b/solution.py
@@ -10,7 +10,7 @@
 MESH = pl.DeviceIdType.MESH
 F32 = jnp.float32
 BF16 = jnp.bfloat16
-NEAR_CHUNK = 4
+NEAR_CHUNK = 8
 
 
 def rows_by_rows(lhs, rhs):

time: 25.8 us -> 25.7 us (level)
  no operation moved by 1% of the time
where the time goes in v6:
time: 25.7 us; the launch traced here: 25.5 us
  Pallas kernels  24.8 us (96%)
  local copies, waits for them, and re-layouts  0.66 us (3%)
    pallas_call x1, Pallas kernels, local(): pl.pallas_call(functools.partial(kernel, n_leaf, n_rhs, plane), out_shape...  24.8 us
    unnamed x1, local copies, waits for them, and re-layouts  0.66 us

profile of v6, /device:TPU:1, one launch (start us, length us, event | category | flops | bytes accessed | tf_op | source)
XLA Modules:
  0.0 25.5 jit_solution(5205907807795605845)
XLA Ops:
  0.0 24.8 %hierarchical_product.1 = f32[16,2048]{1,0:T(8,128)S(1)} custom-call(bf16[16,2048]{1,0:T(8,128)(2,1)} %vectors.1, bf16[4,16,128,128]{3,2,1,0:T(8,128)(2,1)} %near_blocks.1, s32[4,16]{1,0:T(4,128)} %near_src.1, bf16[16,64,128]{2,1,0:T(8,128)(2,1)} %basis.1, bf16[15,64,128]{2,1,0:T(8,128)(2,1)} %local_transfer.1, bf16[16,64,384]{2,1,0:T(8,128)(2,1)} %leaf_coupling.1, ...), custom_call_target="tpu_custom_call" | custom-call | tf_op jit(solution)/shard_map/hierarchical_product/pallas_call | solution.py:620
  24.8 0.7 %copy.12 = f32[16,2048]{1,0:T(8,128)} copy(f32[16,2048]{1,0:T(8,128)S(1)} %hierarchical_product.1) | data formatting | bytes 262144
